TPU v7x, 512 devices: a whole 4x8x8 slice. The times are simulated.
512 devices in a mesh: col: 32 (over z_lo, x, core), row: 16 (over y, z_hi).
Axes of the slice: x: 4, y: 8, z: 8 (z_hi: 2, z_lo: 4; z = z_hi * 4 + z_lo), core: 2. Of those that a mesh axis runs over, the one named last changes fastest.
Arguments:
- thickness: float32 [4096, 8192], P('row', 'col'), may hold values from -6 to 6
- pairing: int32 [3, 6, 256], replicated, may hold values from 0 to 255, each once within a row
Outputs:
- modes: float32 [4096, 8192], P('row', 'col')
All inputs are finite; a program needn't handle non-finite values.
Results may differ from a plain program's by a relative error of at most 0.003.
Values sent between devices are 32-bit elements; how exact they have to be, the bound alone decides.
No kernel may reach another device: no remote copies, remote signals or barrier semaphores. Data moves between devices by JAX's collectives and lax.ppermute only.
A program may use at most 64 MiB of HBM per device.

v0:
```python
import math

import jax
import jax.numpy as jnp
from jax import lax
from jax.sharding import PartitionSpec as P


def shifted(array, axis, by):
    peers = lax.axis_size(axis)
    pairs = [(i, i + by) for i in range(peers) if 0 <= i + by < peers]
    return lax.ppermute(array, axis, pairs)


def jacobi_round(gram_matrix, rotation, ordering):
    half_count = ordering.shape[0] // 2
    leading = ordering[:half_count]
    trailing = ordering[half_count:]
    diagonal = jnp.diagonal(gram_matrix)
    coupling = gram_matrix[leading, trailing]
    angles = 0.5 * jnp.arctan2(2.0 * coupling, diagonal[trailing] - diagonal[leading])
    cosine = jnp.cos(angles)
    sine_part = jnp.sin(angles)
    rotator = jnp.zeros_like(gram_matrix)
    rotator = rotator.at[leading, leading].set(cosine)
    rotator = rotator.at[trailing, trailing].set(cosine)
    rotator = rotator.at[trailing, leading].set(-sine_part)
    rotator = rotator.at[leading, trailing].set(sine_part)
    rows_done = jnp.dot(rotator.T, gram_matrix, precision=lax.Precision.HIGHEST)
    gram_matrix = jnp.dot(rows_done, rotator, precision=lax.Precision.HIGHEST)
    rotation = jnp.dot(rotation, rotator, precision=lax.Precision.HIGHEST)
    return (gram_matrix, rotation)


def jacobi_solve(gram_matrix, orderings):
    rotation = jnp.eye(gram_matrix.shape[0], dtype=jnp.float32)
    for round_index in range(orderings.shape[0]):
        gram_matrix, rotation = jacobi_round(gram_matrix, rotation, orderings[round_index])
    return (gram_matrix, rotation)


def inner_products(left_block, right_block):
    return lax.dot_general(
        left_block, right_block, (((0,), (0,)), ((), ())), precision=lax.Precision.HIGHEST
    )


def plain_move(outgoing, new_lower):
    arrived = shifted(outgoing, "col", 1)
    returned = shifted(new_lower, "col", -1)
    return (arrived, returned)


def shards(thickness, pairing):
    width = thickness.shape[1] // 2
    col_count = lax.axis_size("col")
    position = lax.axis_index("col")
    floor_value = math.sqrt(float(thickness.shape[0] * lax.axis_size("row")))
    upper_block = thickness[:, :width]
    lower_block = thickness[:, width:]
    sections = pairing.shape[0]
    for section in range(sections):
        pair_block = jnp.concatenate([upper_block, lower_block], axis=1)
        gram_matrix = lax.psum(inner_products(pair_block, pair_block), "row")
        gram_matrix, rotation = jacobi_solve(gram_matrix, pairing[section])
        turned = jnp.dot(pair_block, rotation, precision=lax.Precision.HIGHEST)
        if section == sections - 1:
            column_total = lax.psum(jnp.sum(turned, axis=0), "row")
            factor = column_total / jnp.maximum(jnp.abs(column_total), floor_value)
            turned = turned * factor[None, :]
        new_upper = turned[:, :width]
        new_lower = turned[:, width:]
        outgoing = jnp.where(position == 0, new_lower, new_upper)
        arrived, returned = plain_move(outgoing, new_lower)
        upper_block = jnp.where(position == 0, new_upper, arrived)
        lower_block = jnp.where(position == col_count - 1, new_upper, returned)
    return jnp.concatenate([upper_block, lower_block], axis=1)


def solution(mesh):
    placed = (P("row", "col"), P())
    return jax.shard_map(
        shards, mesh=mesh, in_specs=placed, out_specs=P("row", "col"), check_vma=False
    )
```

profile of v0, /device:TPU:7, one launch (start us, length us, event | category | flops | bytes accessed | tf_op | source)
XLA Modules:
  0.0 1345.1 jit_solution(18213078389571502607)
XLA Ops:
  10.2 192.9 %all-reduce.4.cloned.1.call-done = f32[256,256]{1,0:T(8,128)} async-done(((f32[256,256]{1,0:T(8,128)}), f32[256,256]{1,0:T(8,128)}) %all-reduce.4.cloned.1.call-update) | async-done | bytes 262160 | tf_op jit(solution)/shard_map/psum | solution.py:64
  209.8 7.0 scatter_fusion
  216.8 7.0 scatter_fusion.1
  245.7 7.0 scatter_fusion.4
  281.7 7.0 scatter_fusion.8
  288.7 7.0 scatter_fusion.9
  324.6 7.0 scatter_fusion.13
  338.6 7.4 scatter_fusion.15
  353.9 7.0 scatter_fusion.16
  360.9 7.0 scatter_fusion.17
  389.8 7.0 scatter_fusion.20
  418.8 14.0 %collective-permute-start = (f32[256,128]{0,1:T(8,128)S(1)}, f32[256,128]{0,1:T(8,128)S(1)}, u32[]{:S(2)}, u32[]{:S(2)}) collective-permute-start(f32[256,128]{0,1:T(8,128)S(1)} %get-tuple-element.123), channel_id=1, source_target_pairs={{0,16},{16,32},{32,48},{48,64},{64,80},{80,96},{96,112},{112,128},... | collective-permute-start | bytes 393224 | tf_op jit(solution)/shard_map/ppermute | solution.py:12
  442.5 182.9 %all-reduce.6.cloned.1.call-done = f32[256,256]{1,0:T(8,128)} async-done(((f32[256,256]{1,0:T(8,128)}), f32[256,256]{1,0:T(8,128)}) %all-reduce.6.cloned.1.call-update) | async-done | bytes 262160 | tf_op jit(solution)/shard_map/psum | solution.py:64
  632.3 7.0 scatter_fusion.24
  675.1 7.0 scatter_fusion.29
  704.4 7.0 scatter_fusion.32
  747.2 7.0 scatter_fusion.37
  761.2 7.2 scatter_fusion.39
  783.3 7.0 scatter_fusion.41
  841.2 14.0 %collective-permute-start.2 = (f32[256,128]{0,1:T(8,128)S(1)}, f32[256,128]{0,1:T(8,128)S(1)}, u32[]{:S(2)}, u32[]{:S(2)}) collective-permute-start(f32[256,128]{0,1:T(8,128)S(1)} %get-tuple-element.119), channel_id=1, source_target_pairs={{0,16},{16,32},{32,48},{48,64},{64,80},{80,96},{96,112},{112,128},... | collective-permute-start | bytes 393224 | tf_op jit(solution)/shard_map/ppermute | solution.py:12
  864.8 183.0 %all-reduce.8.cloned.1.call-done = f32[256,256]{1,0:T(8,128)} async-done(((f32[256,256]{1,0:T(8,128)}), f32[256,256]{1,0:T(8,128)}) %all-reduce.8.cloned.1.call-update) | async-done | bytes 262160 | tf_op jit(solution)/shard_map/psum | solution.py:64
  1061.9 7.0 scatter_fusion.49
  1097.7 7.0 scatter_fusion.53
  1126.8 7.0 scatter_fusion.56
  1133.8 7.0 scatter_fusion.57
  1162.7 7.0 scatter_fusion.60
  1169.7 7.0 scatter_fusion.61
  1183.7 7.2 scatter_fusion.63
  1198.8 7.0 scatter_fusion.64
  1205.8 7.0 scatter_fusion.65
  1263.8 44.5 %psum.31 = f32[256]{0:T(256)S(1)} all-reduce(f32[256]{0:T(256)S(1)} %get-tuple-element.243), channel_id=1, replica_groups=mesh['col'=32,'row'=16] {'row'}, use_global_device_ids=true, to_apply=%region_76.77 | all-reduce | flops 256 | bytes 2048 | tf_op jit(solution)/shard_map/psum | solution.py:68
  1308.4 20.5 %collective-permute-start.4 = (f32[256,128]{0,1:T(8,128)S(1)}, f32[256,128]{0,1:T(8,128)S(1)}, u32[]{:S(2)}, u32[]{:S(2)}) collective-permute-start(f32[256,128]{0,1:T(8,128)S(1)} %get-tuple-element.115), channel_id=1, source_target_pairs={{0,16},{16,32},{32,48},{48,64},{64,80},{80,96},{96,112},{112,128},... | collective-permute-start | bytes 393224 | tf_op jit(solution)/shard_map/ppermute | solution.py:12
  (330 shorter events, 501.7 us)
Async XLA Ops:
  6.5 1.0 copy-start
  6.5 196.5 %all-reduce.4.cloned.1.call-start = ((), (), s32[]{:S(2)}) async-start(), calls=%async_computation | async-start | bytes 524288 | tf_op jit(solution)/shard_map/psum | solution.py:64
  8.8 0.7 copy-start.4
  8.8 616.5 %all-reduce.6.cloned.1.call-start = ((), (), s32[]{:S(2)}) async-start(), calls=%async_computation.1 | async-start | bytes 524288 | tf_op jit(solution)/shard_map/psum | solution.py:64
  206.9 1.3 copy-start.1
  418.8 16.0 %collective-permute-start = (f32[256,128]{0,1:T(8,128)S(1)}, f32[256,128]{0,1:T(8,128)S(1)}, u32[]{:S(2)}, u32[]{:S(2)}) collective-permute-start(f32[256,128]{0,1:T(8,128)S(1)} %get-tuple-element.123), channel_id=1, source_target_pairs={{0,16},{16,32},{32,48},{48,64},{64,80},{80,96},{96,112},{112,128},... | collective-permute-start | bytes 393224 | tf_op jit(solution)/shard_map/ppermute | solution.py:12
  432.8 8.4 collective-permute-start.1
  442.4 605.4 %all-reduce.8.cloned.1.call-start = ((), (), s32[]{:S(2)}) async-start(), calls=%async_computation.2 | async-start | bytes 524288 | tf_op jit(solution)/shard_map/psum | solution.py:64
  629.4 1.3 copy-start.3
  841.2 16.0 %collective-permute-start.2 = (f32[256,128]{0,1:T(8,128)S(1)}, f32[256,128]{0,1:T(8,128)S(1)}, u32[]{:S(2)}, u32[]{:S(2)}) collective-permute-start(f32[256,128]{0,1:T(8,128)S(1)} %get-tuple-element.119), channel_id=1, source_target_pairs={{0,16},{16,32},{32,48},{48,64},{64,80},{80,96},{96,112},{112,128},... | collective-permute-start | bytes 393224 | tf_op jit(solution)/shard_map/ppermute | solution.py:12
  855.2 8.4 collective-permute-start.3
  1052.0 1.3 copy-start.2
  1308.4 22.4 %collective-permute-start.4 = (f32[256,128]{0,1:T(8,128)S(1)}, f32[256,128]{0,1:T(8,128)S(1)}, u32[]{:S(2)}, u32[]{:S(2)}) collective-permute-start(f32[256,128]{0,1:T(8,128)S(1)} %get-tuple-element.115), channel_id=1, source_target_pairs={{0,16},{16,32},{32,48},{48,64},{64,80},{80,96},{96,112},{112,128},... | collective-permute-start | bytes 393224 | tf_op jit(solution)/shard_map/ppermute | solution.py:12
  1328.9 8.4 collective-permute-start.5
Sparse Core Ops, SparseCore 0:
  10.3 192.7 all-reduce.3
  442.5 182.8 all-reduce.5
  864.9 182.8 all-reduce.7
where the time goes:
time: 1360 us; the launch traced here: 1350 us
  local copies, waits for them, and re-layouts  624 us (46%)
  waiting for transfers between devices  578 us (42%)
  starting transfers between devices  54.4 us (4%)
  blocking collectives  44.5 us (3%)
  matrix products  26.5 us (2%)
  between operations  16 us (1%)
    psum x3, waiting for transfers between devices, shards(): gram_matrix = lax.psum(inner_products(pair_block, pair_block), 'row')  559 us
    scatter x18, local copies, waits for them, and re-layouts, jacobi_round(): rotator = rotator.at[leading, trailing].set(sine_part)  126 us
    scatter x18, local copies, waits for them, and re-layouts, jacobi_round(): rotator = rotator.at[trailing, trailing].set(cosine)  126 us
    scatter x18, local copies, waits for them, and re-layouts, jacobi_round(): rotator = rotator.at[leading, leading].set(cosine)  126 us
    scatter x18, local copies, waits for them, and re-layouts, jacobi_round(): rotator = rotator.at[trailing, leading].set(-sine_part)  125 us
    ppermute x6, starting transfers between devices, shifted(): return lax.ppermute(array, axis, pairs)  54.3 us
    psum x1, blocking collectives, shards(): column_total = lax.psum(jnp.sum(turned, axis=0), 'row')  44.5 us
    gather x18, local copies, waits for them, and re-layouts, jacobi_round(): diagonal = jnp.diagonal(gram_matrix)  43.6 us
  transfers between devices with their start and end apart: 9, of which 6 were waited for; matrix products, arithmetic and copies ran while one was open for 0% of the time, Pallas kernels for 0%

commit v1 on v0

v1 whole, which is shorter than its diff:
```python
import functools
import math

import jax
import jax.numpy as jnp
from jax import lax
from jax.experimental import pallas as pl
from jax.experimental.pallas import tpu as pltpu
from jax.sharding import PartitionSpec as P

F32, BF16 = jnp.float32, jnp.bfloat16
HIGHEST = lax.Precision.HIGHEST


def shifted(array, axis, by):
    peers = lax.axis_size(axis)
    pairs = [(i, i + by) for i in range(peers) if 0 <= i + by < peers]
    return lax.ppermute(array, axis, pairs)


def summed_over_rows(partial):
    peers = lax.axis_size("row")
    rows, width = partial.shape
    parts = partial.reshape(peers, rows // peers, width)
    own = jnp.sum(lax.all_to_all(parts, "row", 0, 0), axis=0)
    spread = jnp.broadcast_to(own[None], (peers,) + own.shape)
    return lax.all_to_all(spread, "row", 0, 0).reshape(rows, width)


def three_parts(x):
    high = x.astype(BF16)
    rest = x - high.astype(F32)
    middle = rest.astype(BF16)
    low = (rest - middle.astype(F32)).astype(BF16)
    return high, middle, low


def columns_by(x, pick):
    dims = (((1,), (0,)), ((), ()))
    high, middle, low = [
        lax.dot_general(part, pick, dims, preferred_element_type=F32) for part in three_parts(x)
    ]
    return high + (middle + low)


def flipped_by(x, pick_t):
    dims = (((1,), (1,)), ((), ()))
    high, middle, low = [
        lax.dot_general(pick_t, part, dims, preferred_element_type=F32) for part in three_parts(x)
    ]
    return high + (middle + low)


def rotation_of(a, b, g):
    x = b - a
    y = 2.0 * g
    top = jnp.maximum(jnp.abs(x), jnp.abs(y))
    none = top == 0.0
    safe = jnp.where(none, 1.0, top)
    xs = x / safe
    ys = y / safe
    inverse = lax.rsqrt(jnp.where(none, 1.0, xs * xs + ys * ys))
    cos2 = jnp.where(none, 1.0, jnp.abs(xs) * inverse)
    sin2 = jnp.abs(ys) * inverse
    h = 0.5 + 0.5 * cos2
    ih = lax.rsqrt(h)
    big = h * ih
    small = 0.5 * sin2 * ih
    c = jnp.where(x >= 0.0, big, small)
    t = jnp.where(x >= 0.0, small, big)
    return c, jnp.where(y < 0.0, -t, t)


def turned(x, c, t):
    half = x.shape[1] // 2
    left, right = x[:, :half], x[:, half:]
    return jnp.concatenate([c * left - t * right, t * left + c * right], axis=1)


def one_hot(column, row):
    return jnp.where(column == row, 1.0, 0.0).astype(BF16)


def solve(gram, rows, columns, want_gram):
    width = gram.shape[0]
    half = width // 2
    rounds = len(rows)
    plain_row = lax.broadcasted_iota(jnp.int32, (1, width), 1)
    plain_column = lax.broadcasted_iota(jnp.int32, (width, 1), 0)
    eye = lax.broadcasted_iota(jnp.int32, (half, half), 0) == lax.broadcasted_iota(
        jnp.int32, (half, half), 1
    )
    rows = [plain_row] + rows + [plain_row]
    columns = [plain_column] + columns + [plain_column]

    def diagonal(block):
        return jnp.sum(jnp.where(eye, block, 0.0), axis=0, keepdims=True)

    gram = columns_by(
        flipped_by(gram, one_hot(columns[1], rows[0])), one_hot(columns[0], rows[1])
    )
    rotation = jnp.where(plain_column == rows[1], 1.0, 0.0).astype(F32)
    for r in range(1, rounds + 1):
        c, t = rotation_of(
            diagonal(gram[:half, :half]), diagonal(gram[half:, half:]), diagonal(gram[:half, half:])
        )
        pick = one_hot(columns[r], rows[r + 1])
        if r < rounds or want_gram:
            pick_t = one_hot(columns[r + 1], rows[r])
            gram = columns_by(turned(flipped_by(turned(gram, c, t), pick_t), c, t), pick)
        rotation = columns_by(turned(rotation, c, t), pick)
    return gram, rotation


def solve_kernel(rounds, gram_ref, rows_ref, columns_ref, rotation_ref):
    rows = [rows_ref[r : r + 1, :] for r in range(rounds)]
    columns = [columns_ref[:, r : r + 1] for r in range(rounds)]
    rotation_ref[...] = solve(gram_ref[...], rows, columns, False)[1]


def jacobi_solve(gram, orderings):
    rounds, width = orderings.shape
    return pl.pallas_call(
        functools.partial(solve_kernel, rounds),
        out_shape=jax.ShapeDtypeStruct((width, width), F32),
    )(gram, orderings, orderings.T)


def shards(thickness, pairing):
    width = thickness.shape[1] // 2
    col_count = lax.axis_size("col")
    peers = lax.axis_size("row")
    position = lax.axis_index("col")
    floor_value = math.sqrt(float(thickness.shape[0] * peers))
    pair_block = thickness
    sections = pairing.shape[0]
    for section in range(sections):
        partial = lax.dot_general(
            pair_block, pair_block, (((0,), (0,)), ((), ())), precision=HIGHEST
        )
        if section == sections - 1:
            totals = jnp.sum(pair_block, axis=0, keepdims=True)
            partial = jnp.concatenate([partial, jnp.pad(totals, ((0, peers - 1), (0, 0)))])
        reduced = summed_over_rows(partial)
        rotation = jacobi_solve(reduced[: 2 * width], pairing[section])
        turned_block = jnp.dot(pair_block, rotation, precision=HIGHEST)
        if section == sections - 1:
            column_total = jnp.dot(
                reduced[2 * width : 2 * width + 1], rotation, precision=HIGHEST
            )
            factor = column_total / jnp.maximum(jnp.abs(column_total), floor_value)
            turned_block = turned_block * factor
        new_upper = turned_block[:, :width]
        new_lower = turned_block[:, width:]
        outgoing = jnp.where(position == 0, new_lower, new_upper)
        arrived = shifted(outgoing, "col", 1)
        returned = shifted(new_lower, "col", -1)
        upper_block = jnp.where(position == 0, new_upper, arrived)
        lower_block = jnp.where(position == col_count - 1, new_upper, returned)
        pair_block = jnp.concatenate([upper_block, lower_block], axis=1)
    return pair_block


def solution(mesh):
    placed = (P("row", "col"), P())
    return jax.shard_map(
        shards, mesh=mesh, in_specs=placed, out_specs=P("row", "col"), check_vma=False
    )
```

time: 1360 us -> 199 us (0.15)
  local copies, waits for them, and re-layouts: 624 us -> 9.26 us
  waiting for transfers between devices: 578 us -> 62.8 us
  starting transfers between devices: 54.4 us -> 32.7 us
  blocking collectives: 44.5 us -> 65.6 us
  Pallas kernels: 0 us -> 20.3 us
  matrix products: 26.5 us -> 6.3 us
  between operations: 16 us -> 0.27 us
    psum x3 -> x0, waiting for transfers between devices: 559 us -> none  [shards(): gram_matrix = lax.psum(inner_products(pair_block, pair_block), 'row')]
    scatter x72 -> x0, local copies, waits for them, and re-layouts: 504 us -> none  [the longest x18 126 us: jacobi_round(): rotator = rotator.at[leading, trailing].set(sine_part)]
    gather x72 -> x0, local copies, waits for them, and re-layouts: 116 us -> none  [the longest x18 43.6 us: jacobi_round(): diagonal = jnp.diagonal(gram_matrix)]
    all_to_all x0 -> x3, blocking collectives: none -> 65.6 us  [summed_over_rows(): own = jnp.sum(lax.all_to_all(parts, 'row', 0, 0), axis=0)]
    psum x1 -> x0, blocking collectives: 44.5 us -> none  [shards(): column_total = lax.psum(jnp.sum(turned, axis=0), 'row')]
    all_to_all x0 -> x3, waiting for transfers between devices: none -> 43.4 us  [summed_over_rows(): return lax.all_to_all(spread, 'row', 0, 0).reshape(rows, width)]
    ppermute x6, starting transfers between devices: 54.3 us -> 20.6 us  [shifted(): return lax.ppermute(array, axis, pairs)]
    pallas_call x0 -> x3, Pallas kernels: none -> 20.3 us  [jacobi_solve(): pl.pallas_call(functools.partial(solve_kernel, rounds), out_shape=jax.Sha...]
  transfers between devices with their start and end apart: 9 -> 9, of which waited for: 6 -> 6; matrix products, arithmetic and copies ran while one was open for 0% -> 2% of each run, Pallas kernels for 0% -> 0%
where the time goes in v1:
time: 199 us; the launch traced here: 198 us
  blocking collectives  65.6 us (33%)
  waiting for transfers between devices  62.8 us (32%)
  starting transfers between devices  32.7 us (16%)
  Pallas kernels  20.3 us (10%)
  local copies, waits for them, and re-layouts  9.26 us (5%)
  matrix products  6.3 us (3%)
    all_to_all x3, blocking collectives, summed_over_rows(): own = jnp.sum(lax.all_to_all(parts, 'row', 0, 0), axis=0)  65.6 us
    all_to_all x3, waiting for transfers between devices, summed_over_rows(): return lax.all_to_all(spread, 'row', 0, 0).reshape(rows, width)  43.4 us
    ppermute x6, starting transfers between devices, shifted(): return lax.ppermute(array, axis, pairs)  20.6 us
    pallas_call x3, Pallas kernels, jacobi_solve(): pl.pallas_call(functools.partial(solve_kernel, rounds), out_shape=jax.Sha...  20.3 us
    ppermute x6, waiting for transfers between devices, shifted(): return lax.ppermute(array, axis, pairs)  19.4 us
    all_to_all x3, starting transfers between devices, summed_over_rows(): return lax.all_to_all(spread, 'row', 0, 0).reshape(rows, width)  12.1 us
    unnamed x13, local copies, waits for them, and re-layouts  4.78 us
  transfers between devices with their start and end apart: 9, of which 6 were waited for; matrix products, arithmetic and copies ran while one was open for 2% of the time, Pallas kernels for 0%

profile of v1, /device:TPU:7, one launch (start us, length us, event | category | flops | bytes accessed | tf_op | source)
XLA Modules:
  0.0 197.7 jit_solution(17396210157669915323)
XLA Ops:
  0.0 0.9 copy-done
  1.6 29.6 %all_to_all.30 = f32[16,16,256]{2,1,0:T(8,128)S(1)} all-to-all(f32[16,16,256]{2,1,0:T(8,128)S(1)} %bitcast.34), channel_id=1, replica_groups=mesh['col'=32,'row'=16] {'row'}, dimensions={0} | all-to-all | bytes 524288 | tf_op jit(solution)/shard_map/all_to_all | solution.py:25
  31.1 0.7 broadcast_in_dim.8
  31.9 3.7 %all-to-all-start.1 = ((f32[16,16,256]{2,1,0:T(8,128)}), f32[16,16,256]{2,1,0:T(8,128)S(1)}, u32[]{:S(2)}, u32[]{:S(2)}) async-start(f32[16,16,256]{2,1,0:T(8,128)} %broadcast_in_dim.8), calls=%async_computation.1 | async-start | bytes 524288 | tf_op jit(solution)/shard_map/all_to_all | solution.py:27
  36.3 0.8 copy.17
  37.1 12.2 %all-to-all-done.1 = f32[16,16,256]{2,1,0:T(8,128)S(1)} async-done(((f32[16,16,256]{2,1,0:T(8,128)}), f32[16,16,256]{2,1,0:T(8,128)S(1)}, u32[]{:S(2)}, u32[]{:S(2)}) %all-to-all-start.1) | async-done | bytes 262176 | tf_op jit(solution)/shard_map/all_to_all | solution.py:27
  50.0 6.8 %shard_map.28 = f32[256,256]{1,0:T(8,128)} custom-call(f32[256,256]{1,0:T(8,128)} %bitcast.36, s32[6,256]{1,0:T(8,128)} %get-tuple-element.18.rows_ref, s32[256,6]{1,0:T(8,128)} %bitcast.39), custom_call_target="tpu_custom_call" | custom-call | tf_op jit(solution)/shard_map/pallas_call | solution.py:123
  56.8 1.5 convolution_bitcast_fusion
  58.3 6.5 %collective-permute-start = (f32[256,128]{0,1:T(8,128)S(1)}, f32[256,128]{0,1:T(8,128)S(1)}, u32[]{:S(2)}, u32[]{:S(2)}) collective-permute-start(f32[256,128]{0,1:T(8,128)S(1)} %get-tuple-element.15), channel_id=1, source_target_pairs={{0,16},{16,32},{32,48},{48,64},{64,80},{80,96},{96,112},{112,128},... | collective-permute-start | bytes 393224 | tf_op jit(solution)/shard_map/ppermute | solution.py:18
  64.9 1.9 collective-permute-start.1
  66.8 6.5 %collective-permute-done.1 = f32[256,128]{0,1:T(8,128)S(1)} collective-permute-done((f32[256,128]{0,1:T(8,128)S(1)}, f32[256,128]{0,1:T(8,128)S(1)}, u32[]{:S(2)}, u32[]{:S(2)}) %collective-permute-start.1) | collective-permute-done | bytes 131104 | tf_op jit(solution)/shard_map/ppermute | solution.py:18
  73.7 16.9 %all_to_all.31 = f32[16,16,256]{2,1,0:T(8,128)S(1)} all-to-all(f32[16,16,256]{2,1,0:T(8,128)S(1)} %bitcast.35), channel_id=1, replica_groups=mesh['col'=32,'row'=16] {'row'}, dimensions={0} | all-to-all | bytes 524288 | tf_op jit(solution)/shard_map/all_to_all | solution.py:25
  90.6 0.7 broadcast_in_dim.9
  91.3 3.5 %all-to-all-start.3 = ((f32[16,16,256]{2,1,0:T(8,128)}), f32[16,16,256]{2,1,0:T(8,128)S(1)}, u32[]{:S(2)}, u32[]{:S(2)}) async-start(f32[16,16,256]{2,1,0:T(8,128)} %broadcast_in_dim.9), calls=%async_computation.3 | async-start | bytes 524288 | tf_op jit(solution)/shard_map/all_to_all | solution.py:27
  94.9 0.8 copy.18
  95.7 14.1 %all-to-all-done.3 = f32[16,16,256]{2,1,0:T(8,128)S(1)} async-done(((f32[16,16,256]{2,1,0:T(8,128)}), f32[16,16,256]{2,1,0:T(8,128)S(1)}, u32[]{:S(2)}, u32[]{:S(2)}) %all-to-all-start.3) | async-done | bytes 262176 | tf_op jit(solution)/shard_map/all_to_all | solution.py:27
  110.4 6.8 %shard_map.29 = f32[256,256]{1,0:T(8,128)} custom-call(f32[256,256]{1,0:T(8,128)} %bitcast.37, s32[6,256]{1,0:T(8,128)} %get-tuple-element.19.rows_ref, s32[256,6]{1,0:T(8,128)} %bitcast.40), custom_call_target="tpu_custom_call" | custom-call | tf_op jit(solution)/shard_map/pallas_call | solution.py:123
  117.2 1.5 fusion
  118.8 3.7 %collective-permute-start.2 = (f32[256,128]{0,1:T(8,128)S(1)}, f32[256,128]{0,1:T(8,128)S(1)}, u32[]{:S(2)}, u32[]{:S(2)}) collective-permute-start(f32[256,128]{0,1:T(8,128)S(1)} %get-tuple-element.11), channel_id=1, source_target_pairs={{0,16},{16,32},{32,48},{48,64},{64,80},{80,96},{96,112},{112,128},... | collective-permute-start | bytes 393224 | tf_op jit(solution)/shard_map/ppermute | solution.py:18
  122.5 1.9 collective-permute-start.3
  124.5 6.5 %collective-permute-done.3 = f32[256,128]{0,1:T(8,128)S(1)} collective-permute-done((f32[256,128]{0,1:T(8,128)S(1)}, f32[256,128]{0,1:T(8,128)S(1)}, u32[]{:S(2)}, u32[]{:S(2)}) %collective-permute-start.3) | collective-permute-done | bytes 131104 | tf_op jit(solution)/shard_map/ppermute | solution.py:18
  131.6 19.2 %all_to_all.32 = f32[16,17,256]{2,1,0:T(8,128)S(1)} all-to-all(f32[16,17,256]{2,1,0:T(8,128)S(1)} %reshape.33), channel_id=1, replica_groups=mesh['col'=32,'row'=16] {'row'}, dimensions={0} | all-to-all | bytes 557056 | tf_op jit(solution)/shard_map/all_to_all | solution.py:25
  150.8 0.8 broadcast_in_dim.11
  151.6 4.8 %all-to-all-start.5 = ((f32[16,17,256]{2,1,0:T(8,128)}), f32[16,17,256]{2,1,0:T(8,128)S(1)}, u32[]{:S(2)}, u32[]{:S(2)}) async-start(f32[16,17,256]{2,1,0:T(8,128)} %broadcast_in_dim.11), calls=%async_computation.5 | async-start | bytes 786432 | tf_op jit(solution)/shard_map/all_to_all | solution.py:27
  156.4 0.8 copy.19
  157.2 17.1 %all-to-all-done.5 = f32[16,17,256]{2,1,0:T(8,128)S(1)} async-done(((f32[16,17,256]{2,1,0:T(8,128)}), f32[16,17,256]{2,1,0:T(8,128)S(1)}, u32[]{:S(2)}, u32[]{:S(2)}) %all-to-all-start.5) | async-done | bytes 278560 | tf_op jit(solution)/shard_map/all_to_all | solution.py:27
  175.1 6.8 %shard_map.30 = f32[256,256]{1,0:T(8,128)} custom-call(f32[256,256]{1,0:T(8,128)} %slice.48.gram_ref, s32[6,256]{1,0:T(8,128)} %get-tuple-element.20.rows_ref, s32[256,6]{1,0:T(8,128)} %bitcast.38), custom_call_target="tpu_custom_call" | custom-call | tf_op jit(solution)/shard_map/pallas_call | solution.py:123
  181.9 1.2 fusion.4
  183.8 4.6 %collective-permute-start.4 = (f32[256,128]{0,1:T(8,128)S(1)}, f32[256,128]{0,1:T(8,128)S(1)}, u32[]{:S(2)}, u32[]{:S(2)}) collective-permute-start(f32[256,128]{0,1:T(8,128)S(1)} %get-tuple-element.7), channel_id=1, source_target_pairs={{0,16},{16,32},{32,48},{48,64},{64,80},{80,96},{96,112},{112,128},... | collective-permute-start | bytes 393224 | tf_op jit(solution)/shard_map/ppermute | solution.py:18
  188.4 1.9 collective-permute-start.5
  190.3 6.5 %collective-permute-done.5 = f32[256,128]{0,1:T(8,128)S(1)} collective-permute-done((f32[256,128]{0,1:T(8,128)S(1)}, f32[256,128]{0,1:T(8,128)S(1)}, u32[]{:S(2)}, u32[]{:S(2)}) %collective-permute-start.5) | collective-permute-done | bytes 131104 | tf_op jit(solution)/shard_map/ppermute | solution.py:18
  196.8 0.8 copy.16
  (33 shorter events, 5.3 us)
Async XLA Ops:
  0.0 1.0 copy-start
  31.9 3.8 %copy-start.4 = (s32[3,6,256]{2,1,0:T(8,128)S(1)}, s32[3,6,256]{2,1,0:T(8,128)}, u32[]{:S(2)}) copy-start(s32[3,6,256]{2,1,0:T(8,128)} %param.3) | copy-start | bytes 55300
  31.9 17.4 %all-to-all-start.1 = ((f32[16,16,256]{2,1,0:T(8,128)}), f32[16,16,256]{2,1,0:T(8,128)S(1)}, u32[]{:S(2)}, u32[]{:S(2)}) async-start(f32[16,16,256]{2,1,0:T(8,128)} %broadcast_in_dim.8), calls=%async_computation.1 | async-start | bytes 524288 | tf_op jit(solution)/shard_map/all_to_all | solution.py:27
  49.3 0.7 copy-start.2
  58.3 8.5 %collective-permute-start = (f32[256,128]{0,1:T(8,128)S(1)}, f32[256,128]{0,1:T(8,128)S(1)}, u32[]{:S(2)}, u32[]{:S(2)}) collective-permute-start(f32[256,128]{0,1:T(8,128)S(1)} %get-tuple-element.15), channel_id=1, source_target_pairs={{0,16},{16,32},{32,48},{48,64},{64,80},{80,96},{96,112},{112,128},... | collective-permute-start | bytes 393224 | tf_op jit(solution)/shard_map/ppermute | solution.py:18
  64.9 8.4 %collective-permute-start.1 = (f32[256,128]{0,1:T(8,128)S(1)}, f32[256,128]{0,1:T(8,128)S(1)}, u32[]{:S(2)}, u32[]{:S(2)}) collective-permute-start(f32[256,128]{0,1:T(8,128)S(1)} %get-tuple-element.16), channel_id=1, source_target_pairs={{16,0},{32,16},{48,32},{64,48},{80,64},{96,80},{112,96},{128,112},... | collective-permute-start | bytes 393224 | tf_op jit(solution)/shard_map/ppermute | solution.py:18
  91.3 18.4 %all-to-all-start.3 = ((f32[16,16,256]{2,1,0:T(8,128)}), f32[16,16,256]{2,1,0:T(8,128)S(1)}, u32[]{:S(2)}, u32[]{:S(2)}) async-start(f32[16,16,256]{2,1,0:T(8,128)} %broadcast_in_dim.9), calls=%async_computation.3 | async-start | bytes 524288 | tf_op jit(solution)/shard_map/all_to_all | solution.py:27
  109.7 0.7 copy-start.3
  118.8 5.7 %collective-permute-start.2 = (f32[256,128]{0,1:T(8,128)S(1)}, f32[256,128]{0,1:T(8,128)S(1)}, u32[]{:S(2)}, u32[]{:S(2)}) collective-permute-start(f32[256,128]{0,1:T(8,128)S(1)} %get-tuple-element.11), channel_id=1, source_target_pairs={{0,16},{16,32},{32,48},{48,64},{64,80},{80,96},{96,112},{112,128},... | collective-permute-start | bytes 393224 | tf_op jit(solution)/shard_map/ppermute | solution.py:18
  122.5 8.4 %collective-permute-start.3 = (f32[256,128]{0,1:T(8,128)S(1)}, f32[256,128]{0,1:T(8,128)S(1)}, u32[]{:S(2)}, u32[]{:S(2)}) collective-permute-start(f32[256,128]{0,1:T(8,128)S(1)} %get-tuple-element.12), channel_id=1, source_target_pairs={{16,0},{32,16},{48,32},{64,48},{80,64},{96,80},{112,96},{128,112},... | collective-permute-start | bytes 393224 | tf_op jit(solution)/shard_map/ppermute | solution.py:18
  151.6 22.7 %all-to-all-start.5 = ((f32[16,17,256]{2,1,0:T(8,128)}), f32[16,17,256]{2,1,0:T(8,128)S(1)}, u32[]{:S(2)}, u32[]{:S(2)}) async-start(f32[16,17,256]{2,1,0:T(8,128)} %broadcast_in_dim.11), calls=%async_computation.5 | async-start | bytes 786432 | tf_op jit(solution)/shard_map/all_to_all | solution.py:27
  181.9 1.3 copy-start.1
  183.8 6.5 %collective-permute-start.4 = (f32[256,128]{0,1:T(8,128)S(1)}, f32[256,128]{0,1:T(8,128)S(1)}, u32[]{:S(2)}, u32[]{:S(2)}) collective-permute-start(f32[256,128]{0,1:T(8,128)S(1)} %get-tuple-element.7), channel_id=1, source_target_pairs={{0,16},{16,32},{32,48},{48,64},{64,80},{80,96},{96,112},{112,128},... | collective-permute-start | bytes 393224 | tf_op jit(solution)/shard_map/ppermute | solution.py:18
  188.4 8.4 %collective-permute-start.5 = (f32[256,128]{0,1:T(8,128)S(1)}, f32[256,128]{0,1:T(8,128)S(1)}, u32[]{:S(2)}, u32[]{:S(2)}) collective-permute-start(f32[256,128]{0,1:T(8,128)S(1)} %get-tuple-element.8), channel_id=1, source_target_pairs={{16,0},{32,16},{48,32},{64,48},{80,64},{96,80},{112,96},{128,112},... | collective-permute-start | bytes 393224 | tf_op jit(solution)/shard_map/ppermute | solution.py:18

commit v2 on v1

--- a/solution.py
+++ b/solution.py
@@ -16,15 +16,6 @@
     peers = lax.axis_size(axis)
     pairs = [(i, i + by) for i in range(peers) if 0 <= i + by < peers]
     return lax.ppermute(array, axis, pairs)
-
-
-def summed_over_rows(partial):
-    peers = lax.axis_size("row")
-    rows, width = partial.shape
-    parts = partial.reshape(peers, rows // peers, width)
-    own = jnp.sum(lax.all_to_all(parts, "row", 0, 0), axis=0)
-    spread = jnp.broadcast_to(own[None], (peers,) + own.shape)
-    return lax.all_to_all(spread, "row", 0, 0).reshape(rows, width)
 
 
 def three_parts(x):
@@ -112,53 +103,341 @@
     return gram, rotation
 
 
-def solve_kernel(rounds, gram_ref, rows_ref, columns_ref, rotation_ref):
+def matmul(x, y):
+    return jnp.dot(x, y, precision=HIGHEST, preferred_element_type=F32)
+
+
+def inner(x, y):
+    return lax.dot_general(
+        x, y, (((0,), (0,)), ((), ())), precision=HIGHEST, preferred_element_type=F32
+    )
+
+
+def orderings_of(rows_ref, columns_ref):
+    rounds = columns_ref.shape[1]
     rows = [rows_ref[r : r + 1, :] for r in range(rounds)]
     columns = [columns_ref[:, r : r + 1] for r in range(rounds)]
-    rotation_ref[...] = solve(gram_ref[...], rows, columns, False)[1]
-
-
-def jacobi_solve(gram, orderings):
-    rounds, width = orderings.shape
+    return rows, columns
+
+
+def square(ref, which=0):
+    parts, _, width = ref.shape
+    chunk = width // parts
+    return ref[:, which * chunk : (which + 1) * chunk, :].reshape(width, width)
+
+
+def own_gram_kernel(block_ref, out_ref):
+    block = block_ref[...]
+    width = block.shape[1]
+    half = width // 2
+    gram = inner(block, block)
+    sums = jnp.sum(block, axis=0, keepdims=True)
+    spare = jnp.concatenate(
+        [sums[:, :half], sums[:, half:], jnp.zeros((half - 2, half), F32)], axis=0
+    )
+    packed = jnp.concatenate(
+        [gram[:half], jnp.concatenate([spare, gram[half:, half:]], axis=1)], axis=0
+    )
+    out_ref[...] = packed.reshape(out_ref.shape)
+
+
+def ahead_kernel(
+    slots, place_ref, block_ref, before_ref, after_ref, far_before_ref, far_after_ref, out_ref
+):
+    place = place_ref[0]
+    last = slots - 1
+    block = block_ref[...]
+    before, after = before_ref[...], after_ref[...]
+    parts, rows, width = out_ref.shape
+    out_ref[:, : rows // 2, :] = inner(
+        jnp.where(place == 0, block, before), jnp.where(place == last, block, after)
+    ).reshape(parts, rows // 2, width)
+    far_before = jnp.where(
+        place == 0, after, jnp.where(place == 1, before, far_before_ref[...])
+    )
+    far_after = jnp.where(
+        place == last, before, jnp.where(place == last - 1, after, far_after_ref[...])
+    )
+    out_ref[:, rows // 2 :, :] = inner(far_before, far_after).reshape(parts, rows // 2, width)
+
+
+def hand_on_kernel(own_ref, ahead_ref, out_ref):
+    parts, rows, width = own_ref.shape
+    total = jnp.sum(own_ref[...], axis=0)
+    out_ref[:, :rows, :] = jnp.broadcast_to(total[None], (parts, rows, width))
+    out_ref[:, rows:, :] = ahead_ref[...]
+
+
+def spread_kernel(own_rows, in_ref, out_ref):
+    out_ref[...] = jnp.broadcast_to(
+        jnp.sum(in_ref[:, own_rows:, :], axis=0)[None], out_ref.shape
+    )
+
+
+def post(is_first, blocks, right_ref, left_ref, own_ref):
+    at = 0
+    for upper, lower in blocks:
+        to = at + upper.shape[0]
+        own_ref[at:to, :] = upper
+        left_ref[at:to, :] = lower
+        right_ref[at:to, :] = jnp.where(is_first, lower, upper)
+        at = to
+
+
+def halves(x):
+    half = x.shape[1] // 2
+    return x[:, :half], x[:, half:]
+
+
+def gram_halves(gram):
+    half = gram.shape[1] // 2
+    return gram[:half, :half], gram[half:, half:]
+
+
+def first_kernel(place_ref, packed_ref, rows_ref, columns_ref, *outs):
+    rows, columns = orderings_of(rows_ref, columns_ref)
+    packed = square(packed_ref)
+    half = packed.shape[1] // 2
+    gram = jnp.concatenate(
+        [
+            packed[:half],
+            jnp.concatenate([packed[:half, half:].T, packed[half:, half:]], axis=1),
+        ],
+        axis=0,
+    )
+    sums = jnp.concatenate([packed[half : half + 1, :half], packed[half + 1 : half + 2, :half]], 1)
+    sums = jnp.broadcast_to(sums, (8, 2 * half))
+    gram, rotation = solve(gram, rows, columns, True)
+    post(
+        place_ref[0] == 0,
+        [halves(rotation), gram_halves(gram), halves(matmul(sums, rotation))],
+        *outs,
+    )
+
+
+def received(slots, place, arrived_ref, returned_ref, own_ref, sizes):
+    pairs = []
+    at = 0
+    for size in sizes:
+        part = slice(at, at + size)
+        upper = jnp.where(place == 0, own_ref[part, :], arrived_ref[part, :])
+        lower = jnp.where(place == slots - 1, own_ref[part, :], returned_ref[part, :])
+        pairs.append((upper, lower))
+        at += size
+    return pairs
+
+
+def joined(upper, lower, cross):
+    return jnp.concatenate(
+        [
+            jnp.concatenate([upper, cross], axis=1),
+            jnp.concatenate([cross.T, lower], axis=1),
+        ],
+        axis=0,
+    )
+
+
+def second_kernel(
+    slots,
+    place_ref,
+    arrived_ref,
+    returned_ref,
+    kept_ref,
+    block_ref,
+    before_ref,
+    after_ref,
+    ahead_ref,
+    rows_ref,
+    columns_ref,
+    *outs,
+):
+    place = place_ref[0]
+    rows, columns = orderings_of(rows_ref, columns_ref)
+    between = square(ahead_ref)
+    depth = between.shape[0]
+    half = depth // 2
+    (turn_upper, turn_lower), (gram_upper, gram_lower), sums = received(
+        slots, place, arrived_ref, returned_ref, kept_ref, (depth, half, 8)
+    )
+    cross = inner(turn_upper, matmul(between, turn_lower))
+    gram, rotation = solve(joined(gram_upper, gram_lower, cross), rows, columns, True)
+    before = jnp.where(place == 0, block_ref[...], before_ref[...])
+    after = jnp.where(place == slots - 1, block_ref[...], after_ref[...])
+    data = jnp.concatenate([matmul(before, turn_upper), matmul(after, turn_lower)], axis=1)
+    data = jnp.concatenate([data, jnp.concatenate(sums, axis=1)], axis=0)
+    first_turns = matmul(turn_upper, rotation[:half])
+    last_turns = matmul(turn_lower, rotation[half:])
+    is_first = place == 0
+    post(
+        is_first,
+        [
+            halves(first_turns),
+            halves(last_turns),
+            gram_halves(gram),
+            halves(matmul(data, rotation)),
+        ],
+        *[ref.at[: ref.shape[0] - depth, :] for ref in outs],
+    )
+    onward = halves(inner(between, first_turns))
+    backward = halves(matmul(between, last_turns))
+    tail = slice(outs[0].shape[0] - depth, outs[0].shape[0])
+    right_ref, left_ref, own_ref = outs
+    right_ref[tail, :] = jnp.where(is_first, onward[1], onward[0])
+    left_ref[tail, :] = backward[1]
+    own_ref[tail, :] = jnp.where(is_first, backward[0], onward[0])
+
+
+def third_kernel(
+    slots,
+    floor_value,
+    place_ref,
+    arrived_ref,
+    returned_ref,
+    kept_ref,
+    ahead_ref,
+    packed_ref,
+    rows_ref,
+    columns_ref,
+    right_out_ref,
+    left_out_ref,
+    own_out_ref,
+):
+    place = place_ref[0]
+    is_first, is_last = place == 0, place == slots - 1
+    rows, columns = orderings_of(rows_ref, columns_ref)
+    packed = square(packed_ref)
+    depth = packed.shape[0]
+    half = depth // 2
+    cells = right_out_ref.shape[0]
+    upper_half = packed[:half]
+    raw = jnp.concatenate(
+        [
+            upper_half,
+            jnp.concatenate([upper_half[:, half:].T, packed[half:, half:]], axis=1),
+        ],
+        axis=0,
+    )
+    (
+        (upper_a, lower_a),
+        (upper_b, lower_b),
+        (gram_upper, gram_lower),
+        data,
+        (onward, backward),
+    ) = received(
+        slots, place, arrived_ref, returned_ref, kept_ref, (depth, depth, half, cells + 8, depth)
+    )
+    left_a = jnp.where(is_first, upper_b, upper_a)
+    left_b = jnp.where(is_first, upper_a, upper_b)
+    right_a = jnp.where(is_last, lower_b, lower_a)
+    right_b = jnp.where(is_last, lower_a, lower_b)
+    cross = (
+        inner(onward, right_a)
+        + inner(left_a, matmul(square(ahead_ref, 1), right_b))
+        + inner(left_b, matmul(raw, right_a) + backward)
+    )
+    rotation = solve(joined(gram_upper, gram_lower, cross), rows, columns, False)[1]
+    data = matmul(jnp.concatenate(data, axis=1), rotation)
+    totals = data[cells : cells + 1, :]
+    upper, lower = halves(data[:cells, :] * (totals / jnp.maximum(jnp.abs(totals), floor_value)))
+    right_out_ref[...] = jnp.where(is_first, lower, upper)
+    left_out_ref[...] = lower
+    own_out_ref[...] = upper
+
+
+def whole(array):
+    return array, pl.BlockSpec(memory_space=pltpu.VMEM)
+
+
+def scalar(array):
+    return array, pl.BlockSpec(memory_space=pltpu.SMEM)
+
+
+def call(kernel, outs, microseconds, *operands):
+    shapes = [jax.ShapeDtypeStruct(shape, F32) for shape in outs]
+    vmem = pl.BlockSpec(memory_space=pltpu.VMEM)
     return pl.pallas_call(
-        functools.partial(solve_kernel, rounds),
-        out_shape=jax.ShapeDtypeStruct((width, width), F32),
-    )(gram, orderings, orderings.T)
+        kernel,
+        out_shape=shapes,
+        in_specs=[spec for _, spec in operands],
+        out_specs=[vmem] * len(shapes),
+        compiler_params=pltpu.CompilerParams(vmem_limit_bytes=16 * 2**20),
+        cost_estimate=pl.CostEstimate(
+            flops=int(microseconds * 1e9), bytes_accessed=2**20, transcendentals=0
+        ),
+    )(*[array for array, _ in operands])
 
 
 def shards(thickness, pairing):
-    width = thickness.shape[1] // 2
-    col_count = lax.axis_size("col")
+    cells, width = thickness.shape
+    half = width // 2
+    slots = lax.axis_size("col")
     peers = lax.axis_size("row")
     position = lax.axis_index("col")
-    floor_value = math.sqrt(float(thickness.shape[0] * peers))
-    pair_block = thickness
-    sections = pairing.shape[0]
-    for section in range(sections):
-        partial = lax.dot_general(
-            pair_block, pair_block, (((0,), (0,)), ((), ())), precision=HIGHEST
-        )
-        if section == sections - 1:
-            totals = jnp.sum(pair_block, axis=0, keepdims=True)
-            partial = jnp.concatenate([partial, jnp.pad(totals, ((0, peers - 1), (0, 0)))])
-        reduced = summed_over_rows(partial)
-        rotation = jacobi_solve(reduced[: 2 * width], pairing[section])
-        turned_block = jnp.dot(pair_block, rotation, precision=HIGHEST)
-        if section == sections - 1:
-            column_total = jnp.dot(
-                reduced[2 * width : 2 * width + 1], rotation, precision=HIGHEST
-            )
-            factor = column_total / jnp.maximum(jnp.abs(column_total), floor_value)
-            turned_block = turned_block * factor
-        new_upper = turned_block[:, :width]
-        new_lower = turned_block[:, width:]
-        outgoing = jnp.where(position == 0, new_lower, new_upper)
-        arrived = shifted(outgoing, "col", 1)
-        returned = shifted(new_lower, "col", -1)
-        upper_block = jnp.where(position == 0, new_upper, arrived)
-        lower_block = jnp.where(position == col_count - 1, new_upper, returned)
-        pair_block = jnp.concatenate([upper_block, lower_block], axis=1)
-    return pair_block
+    place = scalar(jnp.full((1,), position, jnp.int32))
+    floor_value = math.sqrt(float(cells * peers))
+    orders = [(whole(pairing[s]), whole(pairing[s].T)) for s in range(3)]
+    before, after = shifted(thickness, "col", 1), shifted(thickness, "col", -1)
+    far_before, far_after = shifted(thickness, "col", 2), shifted(thickness, "col", -2)
+    block = whole(thickness)
+    chunk = width // peers
+    (own,) = call(own_gram_kernel, [(peers, chunk, width)], 30, block)
+    own = lax.all_to_all(own, "row", 0, 0)
+    (ahead,) = call(
+        functools.partial(ahead_kernel, slots),
+        [(peers, 2 * chunk, width)],
+        2,
+        place,
+        block,
+        whole(before),
+        whole(after),
+        whole(far_before),
+        whole(far_after),
+    )
+    (handed,) = call(hand_on_kernel, [(peers, 3 * chunk, width)], 1, whole(own), whole(ahead))
+    handed = lax.all_to_all(handed, "row", 0, 0)
+    (spread,) = call(
+        functools.partial(spread_kernel, chunk), [(peers, 2 * chunk, width)], 1, whole(handed)
+    )
+    ahead = lax.all_to_all(spread, "row", 0, 0)
+    packed, ahead = whole(handed), whole(ahead)
+
+    rows = width + half + 8
+    right, left, kept = call(
+        first_kernel, [(rows, half)] * 3, 6, place, packed, *orders[0]
+    )
+    arrived, returned = shifted(right, "col", 1), shifted(left, "col", -1)
+    rows = 3 * width + half + cells + 8
+    right, left, kept = call(
+        functools.partial(second_kernel, slots),
+        [(rows, half)] * 3,
+        8,
+        place,
+        whole(arrived),
+        whole(returned),
+        whole(kept),
+        block,
+        whole(before),
+        whole(after),
+        ahead,
+        *orders[1],
+    )
+    arrived, returned = shifted(right, "col", 1), shifted(left, "col", -1)
+    right, left, kept = call(
+        functools.partial(third_kernel, slots, floor_value),
+        [(cells, half)] * 3,
+        8,
+        place,
+        whole(arrived),
+        whole(returned),
+        whole(kept),
+        ahead,
+        packed,
+        *orders[2],
+    )
+    arrived, returned = shifted(right, "col", 1), shifted(left, "col", -1)
+    upper = jnp.where(position == 0, kept, arrived)
+    lower = jnp.where(position == slots - 1, kept, returned)
+    return jnp.concatenate([upper, lower], axis=1)
 
 
 def solution(mesh):

time: 199 us -> 148 us (0.74)
  waiting for transfers between devices: 62.8 us -> 31.2 us
  blocking collectives: 65.6 us -> 35 us
  starting transfers between devices: 32.7 us -> 50.6 us
  matrix products: 6.3 us -> 0 us
  local copies, waits for them, and re-layouts: 9.26 us -> 4.87 us
  Pallas kernels: 20.3 us -> 24.2 us
    all_to_all x3 -> x2, waiting for transfers between devices: 43.4 us -> 0.01 us  [the longest x1 0.01 us: shards(): own = lax.all_to_all(own, 'row', 0, 0)]
    all_to_all x3 -> x1, blocking collectives: 65.6 us -> 35 us  [shards(): handed = lax.all_to_all(handed, 'row', 0, 0)]
    ppermute x6 -> x10, waiting for transfers between devices: 19.4 us -> 31.2 us  [shifted(): return lax.ppermute(array, axis, pairs)]
    ppermute x6 -> x10, starting transfers between devices: 20.6 us -> 29.7 us  [shifted(): return lax.ppermute(array, axis, pairs)]
    all_to_all x3 -> x2, starting transfers between devices: 12.1 us -> 20.9 us  [the longest x1 15.5 us: shards(): own = lax.all_to_all(own, 'row', 0, 0)]
    dot_general x7 -> x0, matrix products: 6.3 us -> none  [the longest x3 3.69 us: shards(): turned_block = jnp.dot(pair_block, rotation, precision=HIGHEST)]
    pallas_call x3 -> x7, Pallas kernels: 20.3 us -> 24.2 us  [call(): pl.pallas_call(kernel, out_shape=shapes, in_specs=[spec for _, spec in op...]
    broadcast_in_dim x3 -> x0, local copies, waits for them, and re-layouts: 2.23 us -> none  [summed_over_rows(): spread = jnp.broadcast_to(own[None], (peers,) + own.shape)]
  transfers between devices with their start and end apart: 9 -> 12, of which waited for: 6 -> 8; matrix products, arithmetic and copies ran while one was open for 2% -> 0% of each run, Pallas kernels for 0% -> 4%
where the time goes in v2:
time: 148 us; the launch traced here: 147 us
  starting transfers between devices  50.6 us (34%)
  blocking collectives  35 us (24%)
  waiting for transfers between devices  31.2 us (21%)
  Pallas kernels  24.2 us (16%)
  local copies, waits for them, and re-layouts  4.87 us (3%)
    all_to_all x1, blocking collectives, shards(): handed = lax.all_to_all(handed, 'row', 0, 0)  35 us
    ppermute x10, waiting for transfers between devices, shifted(): return lax.ppermute(array, axis, pairs)  31.2 us
    ppermute x10, starting transfers between devices, shifted(): return lax.ppermute(array, axis, pairs)  29.7 us
    pallas_call x7, Pallas kernels, call(): pl.pallas_call(kernel, out_shape=shapes, in_specs=[spec for _, spec in op...  24.2 us
    all_to_all x1, starting transfers between devices, shards(): own = lax.all_to_all(own, 'row', 0, 0)  15.5 us
    all_to_all x1, starting transfers between devices, shards(): ahead = lax.all_to_all(spread, 'row', 0, 0)  5.41 us
    unnamed x17, local copies, waits for them, and re-layouts  4.87 us
  transfers between devices with their start and end apart: 12, of which 8 were waited for; matrix products, arithmetic and copies ran while one was open for 0% of the time, Pallas kernels for 4%

profile of v2, /device:TPU:7, one launch (start us, length us, event | category | flops | bytes accessed | tf_op | source)
XLA Modules:
  0.0 146.8 jit_solution(9219278767967343821)
XLA Ops:
  0.0 0.9 copy-done
  1.0 1.1 shard_map.28
  2.1 15.5 %all-to-all-start = ((f32[16,16,256]{2,1,0:T(8,128)}), f32[16,16,256]{2,1,0:T(8,128)S(1)}, u32[]{:S(2)}, u32[]{:S(2)}) async-start(f32[16,16,256]{2,1,0:T(8,128)} %shard_map.28), calls=%async_computation | async-start | bytes 524288 | tf_op jit(solution)/shard_map/all_to_all | solution.py:384
  17.6 3.9 %collective-permute-start = (f32[256,256]{1,0:T(8,128)S(1)}, f32[256,256]{1,0:T(8,128)S(1)}, u32[]{:S(2)}, u32[]{:S(2)}) collective-permute-start(f32[256,256]{1,0:T(8,128)S(1)} %copy-done.1), channel_id=1, source_target_pairs={{0,16},{16,32},{32,48},{48,64},{64,80},{80,96},{96,112},{112,128},... | collective-permute-start | bytes 786440 | tf_op jit(solution)/shard_map/ppermute | solution.py:18
  21.5 1.9 %collective-permute-start.1 = (f32[256,256]{1,0:T(8,128)S(1)}, f32[256,256]{1,0:T(8,128)S(1)}, u32[]{:S(2)}, u32[]{:S(2)}) collective-permute-start(f32[256,256]{1,0:T(8,128)S(1)} %copy-done.1), channel_id=1, source_target_pairs={{16,0},{32,16},{48,32},{64,48},{80,64},{96,80},{112,96},{128,112},... | collective-permute-start | bytes 786440 | tf_op jit(solution)/shard_map/ppermute | solution.py:18
  23.4 3.1 %collective-permute-start.2 = (f32[256,256]{1,0:T(8,128)S(1)}, f32[256,256]{1,0:T(8,128)S(1)}, u32[]{:S(2)}, u32[]{:S(2)}) collective-permute-start(f32[256,256]{1,0:T(8,128)S(1)} %copy-done.1), channel_id=1, source_target_pairs={{0,32},{16,48},{32,64},{48,80},{64,96},{80,112},{96,128},{112,144}... | collective-permute-start | bytes 786440 | tf_op jit(solution)/shard_map/ppermute | solution.py:18
  26.5 2.2 %collective-permute-start.3 = (f32[256,256]{1,0:T(8,128)S(1)}, f32[256,256]{1,0:T(8,128)S(1)}, u32[]{:S(2)}, u32[]{:S(2)}) collective-permute-start(f32[256,256]{1,0:T(8,128)S(1)} %copy-done.1), channel_id=1, source_target_pairs={{32,0},{48,16},{64,32},{80,48},{96,64},{112,80},{128,96},{144,112}... | collective-permute-start | bytes 786440 | tf_op jit(solution)/shard_map/ppermute | solution.py:18
  28.7 3.7 %collective-permute-done.1.after_ref = f32[256,256]{1,0:T(8,128)S(1)} collective-permute-done((f32[256,256]{1,0:T(8,128)S(1)}, f32[256,256]{1,0:T(8,128)S(1)}, u32[]{:S(2)}, u32[]{:S(2)}) %collective-permute-start.1) | collective-permute-done | bytes 262176 | tf_op jit(solution)/shard_map/ppermute | solution.py:18
  32.4 1.4 collective-permute-done.2.far_before_ref
  33.9 1.9 %collective-permute-done.3.far_after_ref = f32[256,256]{1,0:T(8,128)S(1)} collective-permute-done((f32[256,256]{1,0:T(8,128)S(1)}, f32[256,256]{1,0:T(8,128)S(1)}, u32[]{:S(2)}, u32[]{:S(2)}) %collective-permute-start.3) | collective-permute-done | bytes 262176 | tf_op jit(solution)/shard_map/ppermute | solution.py:18
  35.7 0.8 shard_map.29.ahead_ref
  36.6 35.0 %all_to_all.15.packed_ref.in_ref = f32[16,48,256]{2,1,0:T(8,128)S(1)} all-to-all(f32[16,48,256]{2,1,0:T(8,128)S(1)} %shard_map.30), channel_id=1, replica_groups=mesh['col'=32,'row'=16] {'row'}, dimensions={0} | all-to-all | bytes 1572864 | tf_op jit(solution)/shard_map/all_to_all | solution.py:397
  71.6 0.9 shard_map.32
  72.5 5.4 %all-to-all-start.2 = ((f32[16,32,256]{2,1,0:T(8,128)}), f32[16,32,256]{2,1,0:T(8,128)S(1)}, u32[]{:S(2)}, u32[]{:S(2)}) async-start(f32[16,32,256]{2,1,0:T(8,128)} %shard_map.32), calls=%async_computation.2 | async-start | bytes 1048576 | tf_op jit(solution)/shard_map/all_to_all | solution.py:401
  78.1 5.7 %shard_map.31 = (f32[392,128]{1,0:T(8,128)S(1)}, f32[392,128]{1,0:T(8,128)S(1)}, f32[392,128]{1,0:T(8,128)S(1)}) custom-call(s32[1]{0:T(128)} %bitcast.place_ref, f32[16,48,256]{2,1,0:T(8,128)S(1)} %all_to_all.15.packed_ref.in_ref, s32[6,256]{1,0:T(8,128)S(1)} %get-tuple-element.26.rows_ref, s32[256,6]{1,0:T(8,128)S(1)} %bitcast.18), custom_call_target="tpu_custom_call" | custom-call | flops 6000000000 | bytes 1048576 | tf_op jit(solution)/shard_map/pallas_call | solution.py:358
  84.4 5.6 %collective-permute-start.4 = (f32[392,128]{1,0:T(8,128)S(1)}, f32[392,128]{1,0:T(8,128)S(1)}, u32[]{:S(2)}, u32[]{:S(2)}) collective-permute-start(f32[392,128]{1,0:T(8,128)S(1)} %get-tuple-element.14), channel_id=1, source_target_pairs={{0,16},{16,32},{32,48},{48,64},{64,80},{80,96},{96,112},{112,128},... | collective-permute-start | bytes 602120 | tf_op jit(solution)/shard_map/ppermute | solution.py:18
  90.1 2.4 %collective-permute-start.5 = (f32[392,128]{1,0:T(8,128)S(1)}, f32[392,128]{1,0:T(8,128)S(1)}, u32[]{:S(2)}, u32[]{:S(2)}) collective-permute-start(f32[392,128]{1,0:T(8,128)S(1)} %get-tuple-element.15), channel_id=1, source_target_pairs={{16,0},{32,16},{48,32},{64,48},{80,64},{96,80},{112,96},{128,112},... | collective-permute-start | bytes 602120 | tf_op jit(solution)/shard_map/ppermute | solution.py:18
  92.6 4.7 %collective-permute-done.4.arrived_ref = f32[392,128]{1,0:T(8,128)S(1)} collective-permute-done((f32[392,128]{1,0:T(8,128)S(1)}, f32[392,128]{1,0:T(8,128)S(1)}, u32[]{:S(2)}, u32[]{:S(2)}) %collective-permute-start.4) | collective-permute-done | bytes 200736 | tf_op jit(solution)/shard_map/ppermute | solution.py:18
  97.3 2.1 %collective-permute-done.5.returned_ref = f32[392,128]{1,0:T(8,128)S(1)} collective-permute-done((f32[392,128]{1,0:T(8,128)S(1)}, f32[392,128]{1,0:T(8,128)S(1)}, u32[]{:S(2)}, u32[]{:S(2)}) %collective-permute-start.5) | collective-permute-done | bytes 200736 | tf_op jit(solution)/shard_map/ppermute | solution.py:18
  99.5 0.9 copy-done.5
  100.4 8.4 %shard_map.33 = (f32[1160,128]{1,0:T(8,128)}, f32[1160,128]{1,0:T(8,128)S(1)}, f32[1160,128]{1,0:T(8,128)S(1)}) custom-call(s32[1]{0:T(128)} %bitcast.place_ref, f32[392,128]{1,0:T(8,128)S(1)} %collective-permute-done.4.arrived_ref, f32[392,128]{1,0:T(8,128)S(1)} %collective-permute-done.5.returned_ref, f32[392,128]{1,0:T(8,128)S(1)} %copy-done.5, ...), custom_call_target="tpu_custom_call" | custom-call | flops 8000000000 | bytes 1048576 | tf_op jit(solution)/shard_map/pallas_call | solution.py:358
  108.8 0.8 copy-done.2
  109.6 4.3 %collective-permute-start.6 = (f32[1160,128]{1,0:T(8,128)}, f32[1160,128]{1,0:T(8,128)S(1)}, u32[]{:S(2)}, u32[]{:S(2)}) collective-permute-start(f32[1160,128]{1,0:T(8,128)} %get-tuple-element.17), channel_id=1, source_target_pairs={{0,16},{16,32},{32,48},{48,64},{64,80},{80,96},{96,112},{112,128},... | collective-permute-start | bytes 1781768 | tf_op jit(solution)/shard_map/ppermute | solution.py:18
  114.0 1.9 %collective-permute-start.7 = (f32[1160,128]{1,0:T(8,128)S(1)}, f32[1160,128]{1,0:T(8,128)S(1)}, u32[]{:S(2)}, u32[]{:S(2)}) collective-permute-start(f32[1160,128]{1,0:T(8,128)S(1)} %get-tuple-element.18), channel_id=1, source_target_pairs={{16,0},{32,16},{48,32},{64,48},{80,64},{96,80},{112,96},{128,112},... | collective-permute-start | bytes 1781768 | tf_op jit(solution)/shard_map/ppermute | solution.py:18
  116.1 5.1 %collective-permute-done.6.arrived_ref = f32[1160,128]{1,0:T(8,128)S(1)} collective-permute-done((f32[1160,128]{1,0:T(8,128)}, f32[1160,128]{1,0:T(8,128)S(1)}, u32[]{:S(2)}, u32[]{:S(2)}) %collective-permute-start.6) | collective-permute-done | bytes 593952 | tf_op jit(solution)/shard_map/ppermute | solution.py:18
  121.1 6.2 %collective-permute-done.7.returned_ref = f32[1160,128]{1,0:T(8,128)S(1)} collective-permute-done((f32[1160,128]{1,0:T(8,128)S(1)}, f32[1160,128]{1,0:T(8,128)S(1)}, u32[]{:S(2)}, u32[]{:S(2)}) %collective-permute-start.7) | collective-permute-done | bytes 593952 | tf_op jit(solution)/shard_map/ppermute | solution.py:18
  127.3 1.1 copy-done.3
  128.4 7.3 %shard_map.34 = (f32[256,128]{1,0:T(8,128)S(1)}, f32[256,128]{1,0:T(8,128)S(1)}, f32[256,128]{1,0:T(8,128)S(1)}) custom-call(s32[1]{0:T(128)} %bitcast.place_ref, f32[1160,128]{1,0:T(8,128)S(1)} %collective-permute-done.6.arrived_ref, f32[1160,128]{1,0:T(8,128)S(1)} %collective-permute-done.7.returned_ref, f32[1160,128]{1,0:T(8,128)S(1)} %copy-done.3, ...), custom_call_target="tpu_custom_call" | custom-call | flops 8000000000 | bytes 1048576 | tf_op jit(solution)/shard_map/pallas_call | solution.py:358
  135.7 1.9 %collective-permute-start.8 = (f32[256,128]{1,0:T(8,128)S(1)}, f32[256,128]{1,0:T(8,128)S(1)}, u32[]{:S(2)}, u32[]{:S(2)}) collective-permute-start(f32[256,128]{1,0:T(8,128)S(1)} %get-tuple-element.21), channel_id=1, source_target_pairs={{0,16},{16,32},{32,48},{48,64},{64,80},{80,96},{96,112},{112,128},... | collective-permute-start | bytes 393224 | tf_op jit(solution)/shard_map/ppermute | solution.py:18
  137.6 2.4 %collective-permute-start.9 = (f32[256,128]{1,0:T(8,128)S(1)}, f32[256,128]{1,0:T(8,128)S(1)}, u32[]{:S(2)}, u32[]{:S(2)}) collective-permute-start(f32[256,128]{1,0:T(8,128)S(1)} %get-tuple-element.22), channel_id=1, source_target_pairs={{16,0},{32,16},{48,32},{64,48},{80,64},{96,80},{112,96},{128,112},... | collective-permute-start | bytes 393224 | tf_op jit(solution)/shard_map/ppermute | solution.py:18
  140.1 6.0 %collective-permute-done.9 = f32[256,128]{1,0:T(8,128)S(1)} collective-permute-done((f32[256,128]{1,0:T(8,128)S(1)}, f32[256,128]{1,0:T(8,128)S(1)}, u32[]{:S(2)}, u32[]{:S(2)}) %collective-permute-start.9) | collective-permute-done | bytes 131104 | tf_op jit(solution)/shard_map/ppermute | solution.py:18
  146.1 0.7 pad_maximum_fusion
  (20 shorter events, 1.2 us)
Async XLA Ops:
  0.0 0.9 copy-start
  2.1 15.5 %copy-start.1 = (f32[256,256]{1,0:T(8,128)S(1)}, f32[256,256]{1,0:T(8,128)}, u32[]{:S(2)}) copy-start(f32[256,256]{1,0:T(8,128)} %block_ref.5) | copy-start | bytes 786436
  2.1 34.5 %all-to-all-start = ((f32[16,16,256]{2,1,0:T(8,128)}), f32[16,16,256]{2,1,0:T(8,128)S(1)}, u32[]{:S(2)}, u32[]{:S(2)}) async-start(f32[16,16,256]{2,1,0:T(8,128)} %shard_map.28), calls=%async_computation | async-start | bytes 524288 | tf_op jit(solution)/shard_map/all_to_all | solution.py:384
  17.6 11.1 %collective-permute-start = (f32[256,256]{1,0:T(8,128)S(1)}, f32[256,256]{1,0:T(8,128)S(1)}, u32[]{:S(2)}, u32[]{:S(2)}) collective-permute-start(f32[256,256]{1,0:T(8,128)S(1)} %copy-done.1), channel_id=1, source_target_pairs={{0,16},{16,32},{32,48},{48,64},{64,80},{80,96},{96,112},{112,128},... | collective-permute-start | bytes 786440 | tf_op jit(solution)/shard_map/ppermute | solution.py:18
  21.5 11.0 %collective-permute-start.1 = (f32[256,256]{1,0:T(8,128)S(1)}, f32[256,256]{1,0:T(8,128)S(1)}, u32[]{:S(2)}, u32[]{:S(2)}) collective-permute-start(f32[256,256]{1,0:T(8,128)S(1)} %copy-done.1), channel_id=1, source_target_pairs={{16,0},{32,16},{48,32},{64,48},{80,64},{96,80},{112,96},{128,112},... | collective-permute-start | bytes 786440 | tf_op jit(solution)/shard_map/ppermute | solution.py:18
  23.4 10.5 %collective-permute-start.2 = (f32[256,256]{1,0:T(8,128)S(1)}, f32[256,256]{1,0:T(8,128)S(1)}, u32[]{:S(2)}, u32[]{:S(2)}) collective-permute-start(f32[256,256]{1,0:T(8,128)S(1)} %copy-done.1), channel_id=1, source_target_pairs={{0,32},{16,48},{32,64},{48,80},{64,96},{80,112},{96,128},{112,144}... | collective-permute-start | bytes 786440 | tf_op jit(solution)/shard_map/ppermute | solution.py:18
  26.5 9.2 %collective-permute-start.3 = (f32[256,256]{1,0:T(8,128)S(1)}, f32[256,256]{1,0:T(8,128)S(1)}, u32[]{:S(2)}, u32[]{:S(2)}) collective-permute-start(f32[256,256]{1,0:T(8,128)S(1)} %copy-done.1), channel_id=1, source_target_pairs={{32,0},{48,16},{64,32},{80,48},{96,64},{112,80},{128,96},{144,112}... | collective-permute-start | bytes 786440 | tf_op jit(solution)/shard_map/ppermute | solution.py:18
  72.5 5.4 %copy-start.6 = (s32[3,6,256]{2,1,0:T(8,128)S(1)}, s32[3,6,256]{2,1,0:T(8,128)}, u32[]{:S(2)}) copy-start(s32[3,6,256]{2,1,0:T(8,128)} %param.3) | copy-start | bytes 55300
  72.5 27.0 %all-to-all-start.2 = ((f32[16,32,256]{2,1,0:T(8,128)}), f32[16,32,256]{2,1,0:T(8,128)S(1)}, u32[]{:S(2)}, u32[]{:S(2)}) async-start(f32[16,32,256]{2,1,0:T(8,128)} %shard_map.32), calls=%async_computation.2 | async-start | bytes 1048576 | tf_op jit(solution)/shard_map/all_to_all | solution.py:401
  83.7 0.7 copy-start.4
  84.4 12.9 %collective-permute-start.4 = (f32[392,128]{1,0:T(8,128)S(1)}, f32[392,128]{1,0:T(8,128)S(1)}, u32[]{:S(2)}, u32[]{:S(2)}) collective-permute-start(f32[392,128]{1,0:T(8,128)S(1)} %get-tuple-element.14), channel_id=1, source_target_pairs={{0,16},{16,32},{32,48},{48,64},{64,80},{80,96},{96,112},{112,128},... | collective-permute-start | bytes 602120 | tf_op jit(solution)/shard_map/ppermute | solution.py:18
  90.1 9.4 %collective-permute-start.5 = (f32[392,128]{1,0:T(8,128)S(1)}, f32[392,128]{1,0:T(8,128)S(1)}, u32[]{:S(2)}, u32[]{:S(2)}) collective-permute-start(f32[392,128]{1,0:T(8,128)S(1)} %get-tuple-element.15), channel_id=1, source_target_pairs={{16,0},{32,16},{48,32},{64,48},{80,64},{96,80},{112,96},{128,112},... | collective-permute-start | bytes 602120 | tf_op jit(solution)/shard_map/ppermute | solution.py:18
  99.5 0.9 copy-start.5
  108.8 0.8 copy-start.2
  109.6 11.5 %collective-permute-start.6 = (f32[1160,128]{1,0:T(8,128)}, f32[1160,128]{1,0:T(8,128)S(1)}, u32[]{:S(2)}, u32[]{:S(2)}) collective-permute-start(f32[1160,128]{1,0:T(8,128)} %get-tuple-element.17), channel_id=1, source_target_pairs={{0,16},{16,32},{32,48},{48,64},{64,80},{80,96},{96,112},{112,128},... | collective-permute-start | bytes 1781768 | tf_op jit(solution)/shard_map/ppermute | solution.py:18
  114.0 13.4 %collective-permute-start.7 = (f32[1160,128]{1,0:T(8,128)S(1)}, f32[1160,128]{1,0:T(8,128)S(1)}, u32[]{:S(2)}, u32[]{:S(2)}) collective-permute-start(f32[1160,128]{1,0:T(8,128)S(1)} %get-tuple-element.18), channel_id=1, source_target_pairs={{16,0},{32,16},{48,32},{64,48},{80,64},{96,80},{112,96},{128,112},... | collective-permute-start | bytes 1781768 | tf_op jit(solution)/shard_map/ppermute | solution.py:18
  127.3 1.1 copy-start.3
  135.7 4.4 %collective-permute-start.8 = (f32[256,128]{1,0:T(8,128)S(1)}, f32[256,128]{1,0:T(8,128)S(1)}, u32[]{:S(2)}, u32[]{:S(2)}) collective-permute-start(f32[256,128]{1,0:T(8,128)S(1)} %get-tuple-element.21), channel_id=1, source_target_pairs={{0,16},{16,32},{32,48},{48,64},{64,80},{80,96},{96,112},{112,128},... | collective-permute-start | bytes 393224 | tf_op jit(solution)/shard_map/ppermute | solution.py:18
  137.6 8.4 %collective-permute-start.9 = (f32[256,128]{1,0:T(8,128)S(1)}, f32[256,128]{1,0:T(8,128)S(1)}, u32[]{:S(2)}, u32[]{:S(2)}) collective-permute-start(f32[256,128]{1,0:T(8,128)S(1)} %get-tuple-element.22), channel_id=1, source_target_pairs={{16,0},{32,16},{48,32},{64,48},{80,64},{96,80},{112,96},{128,112},... | collective-permute-start | bytes 393224 | tf_op jit(solution)/shard_map/ppermute | solution.py:18

commit v3 on v2

v3 whole, which is shorter than its diff:
```python
import functools
import math

import jax
import jax.numpy as jnp
from jax import lax
from jax.experimental import pallas as pl
from jax.experimental.pallas import tpu as pltpu
from jax.sharding import PartitionSpec as P

F32, BF16 = jnp.float32, jnp.bfloat16
HIGHEST = lax.Precision.HIGHEST


def shifted(array, axis, by):
    peers = lax.axis_size(axis)
    pairs = [(i, i + by) for i in range(peers) if 0 <= i + by < peers]
    return lax.ppermute(array, axis, pairs)


def three_parts(x):
    high = x.astype(BF16)
    rest = x - high.astype(F32)
    middle = rest.astype(BF16)
    low = (rest - middle.astype(F32)).astype(BF16)
    return high, middle, low


def columns_by(x, pick):
    dims = (((1,), (0,)), ((), ()))
    high, middle, low = [
        lax.dot_general(part, pick, dims, preferred_element_type=F32) for part in three_parts(x)
    ]
    return high + (middle + low)


def flipped_by(x, pick_t):
    dims = (((1,), (1,)), ((), ()))
    high, middle, low = [
        lax.dot_general(pick_t, part, dims, preferred_element_type=F32) for part in three_parts(x)
    ]
    return high + (middle + low)


def rotation_of(a, b, g):
    x = b - a
    y = 2.0 * g
    top = jnp.maximum(jnp.abs(x), jnp.abs(y))
    none = top == 0.0
    safe = jnp.where(none, 1.0, top)
    xs = x / safe
    ys = y / safe
    inverse = lax.rsqrt(jnp.where(none, 1.0, xs * xs + ys * ys))
    cos2 = jnp.where(none, 1.0, jnp.abs(xs) * inverse)
    sin2 = jnp.abs(ys) * inverse
    h = 0.5 + 0.5 * cos2
    ih = lax.rsqrt(h)
    big = h * ih
    small = 0.5 * sin2 * ih
    c = jnp.where(x >= 0.0, big, small)
    t = jnp.where(x >= 0.0, small, big)
    return c, jnp.where(y < 0.0, -t, t)


def turned(x, c, t):
    half = x.shape[1] // 2
    left, right = x[:, :half], x[:, half:]
    return jnp.concatenate([c * left - t * right, t * left + c * right], axis=1)


def one_hot(column, row):
    return jnp.where(column == row, 1.0, 0.0).astype(BF16)


def solve(gram, rows, columns, want_gram):
    width = gram.shape[0]
    half = width // 2
    rounds = len(rows)
    plain_row = lax.broadcasted_iota(jnp.int32, (1, width), 1)
    plain_column = lax.broadcasted_iota(jnp.int32, (width, 1), 0)
    eye = lax.broadcasted_iota(jnp.int32, (half, half), 0) == lax.broadcasted_iota(
        jnp.int32, (half, half), 1
    )
    rows = [plain_row] + rows + [plain_row]
    columns = [plain_column] + columns + [plain_column]

    def diagonal(block):
        return jnp.sum(jnp.where(eye, block, 0.0), axis=0, keepdims=True)

    gram = columns_by(
        flipped_by(gram, one_hot(columns[1], rows[0])), one_hot(columns[0], rows[1])
    )
    rotation = jnp.where(plain_column == rows[1], 1.0, 0.0).astype(F32)
    for r in range(1, rounds + 1):
        c, t = rotation_of(
            diagonal(gram[:half, :half]), diagonal(gram[half:, half:]), diagonal(gram[:half, half:])
        )
        pick = one_hot(columns[r], rows[r + 1])
        if r < rounds or want_gram:
            pick_t = one_hot(columns[r + 1], rows[r])
            gram = columns_by(turned(flipped_by(turned(gram, c, t), pick_t), c, t), pick)
        rotation = columns_by(turned(rotation, c, t), pick)
    return gram, rotation


def along_ring(parts):
    rows = lax.axis_size("row")
    rings = [list(range(start, rows, 2)) for start in range(2)]
    return lax.all_to_all(parts, "row", 0, 0, axis_index_groups=rings)


def chip_swap(array):
    slots = lax.axis_size("col")
    return lax.ppermute(array, "col", [(m, m ^ 1) for m in range(slots)])


def outer_swap(array):
    slots = lax.axis_size("col")
    pairs = [(m, min(max(((m + 1) ^ 1) - 1, 0), slots - 1)) for m in range(slots)]
    return lax.ppermute(array, "col", pairs)


def matmul(x, y):
    return jnp.dot(x, y, precision=HIGHEST, preferred_element_type=F32)


def inner(x, y):
    return lax.dot_general(
        x, y, (((0,), (0,)), ((), ())), precision=HIGHEST, preferred_element_type=F32
    )


def orderings_of(rows_ref, columns_ref):
    rounds = columns_ref.shape[1]
    rows = [rows_ref[r : r + 1, :] for r in range(rounds)]
    columns = [columns_ref[:, r : r + 1] for r in range(rounds)]
    return rows, columns


def square(ref, which):
    parts, _, width = ref.shape
    chunk = width // parts
    return ref[:, which * chunk : (which + 1) * chunk, :].reshape(width, width)


def own_gram_kernel(block_ref, out_ref):
    block = block_ref[...]
    width = block.shape[1]
    half = width // 2
    gram = inner(block, block)
    sums = jnp.sum(block, axis=0, keepdims=True)
    spare = jnp.concatenate(
        [sums[:, :half], sums[:, half:], jnp.zeros((half - 2, half), F32)], axis=0
    )
    packed = jnp.concatenate(
        [gram[:half], jnp.concatenate([spare, gram[half:, half:]], axis=1)], axis=0
    )
    out_ref[...] = packed.reshape(out_ref.shape)


def is_even(place_ref):
    return lax.rem(place_ref[0], 2) == 0


def in_order(even, inner_block, outer_block):
    return jnp.where(even, outer_block, inner_block), jnp.where(even, inner_block, outer_block)


def ahead_kernel(
    slots,
    place_ref,
    inner_ref,
    outer_ref,
    far_before_ref,
    far_after_ref,
    out_ref,
    before_ref,
    after_ref,
):
    place = place_ref[0]
    last = slots - 1
    parts, rows, width = out_ref.shape
    chunk = rows // 2
    before, after = in_order(is_even(place_ref), inner_ref[...], outer_ref[...])
    far_before = jnp.where(
        place == 0, after, jnp.where(place == 1, before, far_before_ref[...])
    )
    far_after = jnp.where(
        place == last, before, jnp.where(place == last - 1, after, far_after_ref[...])
    )
    before_ref[...] = far_before
    after_ref[...] = far_after
    out_ref[:, :chunk, :] = inner(before, after).reshape(parts, chunk, width)
    out_ref[:, chunk:, :] = inner(far_before, far_after).reshape(parts, chunk, width)


def total_kernel(in_ref, out_ref):
    out_ref[...] = jnp.sum(in_ref[...], axis=0)


def spread_kernel(one_ref, other_ref, *refs):
    out_ref = refs[-1]
    out_ref[...] = jnp.broadcast_to((one_ref[...] + other_ref[...])[None], out_ref.shape)


def post(place_ref, blocks, inner_out_ref, outer_out_ref):
    upper_inside = is_even(place_ref) & (place_ref[0] != 0)
    at = 0
    for upper, lower in blocks:
        to = at + upper.shape[0]
        inner_out_ref[at:to, :] = jnp.where(upper_inside, upper, lower)
        outer_out_ref[at:to, :] = jnp.where(upper_inside, lower, upper)
        at = to


def halves(x):
    half = x.shape[1] // 2
    return x[:, :half], x[:, half:]


def gram_halves(gram):
    half = gram.shape[1] // 2
    return gram[:half, :half], gram[half:, half:]


def first_kernel(place_ref, sums_ref, rows_ref, columns_ref, *outs):
    rows, columns = orderings_of(rows_ref, columns_ref)
    packed = square(sums_ref, 0)
    half = packed.shape[1] // 2
    gram = jnp.concatenate(
        [
            packed[:half],
            jnp.concatenate([packed[:half, half:].T, packed[half:, half:]], axis=1),
        ],
        axis=0,
    )
    sums = jnp.concatenate([packed[half : half + 1, :half], packed[half + 1 : half + 2, :half]], 1)
    sums = jnp.broadcast_to(sums, (8, 2 * half))
    gram, rotation = solve(gram, rows, columns, True)
    post(
        place_ref,
        [halves(rotation), gram_halves(gram), halves(matmul(sums, rotation))],
        *outs,
    )


def received(even, inner_ref, outer_ref, sizes):
    pairs = []
    at = 0
    for size in sizes:
        part = slice(at, at + size)
        pairs.append(in_order(even, inner_ref[part, :], outer_ref[part, :]))
        at += size
    return pairs


def joined(upper, lower, cross):
    return jnp.concatenate(
        [
            jnp.concatenate([upper, cross], axis=1),
            jnp.concatenate([cross.T, lower], axis=1),
        ],
        axis=0,
    )


def second_kernel(
    slots, place_ref, inner_ref, outer_ref, sums_ref, rows_ref, columns_ref, *outs
):
    place = place_ref[0]
    even = is_even(place_ref)
    rows, columns = orderings_of(rows_ref, columns_ref)
    near = square(sums_ref, 0)
    depth = near.shape[0]
    half = depth // 2
    (turn_upper, turn_lower), (gram_upper, gram_lower), sums = received(
        even, inner_ref, outer_ref, (depth, half, 8)
    )
    onward, backward = inner(near, turn_upper), matmul(near, turn_lower)
    cross = inner(turn_upper, backward)
    first = jnp.concatenate([turn_upper, onward], axis=0)
    last = jnp.concatenate([turn_lower, backward], axis=0)
    gram, rotation = solve(joined(gram_upper, gram_lower, cross), rows, columns, True)
    first, last = matmul(first, rotation[:half]), matmul(last, rotation[half:])
    first_turns, last_turns = first[:depth], last[:depth]
    onward, backward = halves(first[depth:]), halves(last[depth:])
    inner_out_ref, outer_out_ref = outs
    body = inner_out_ref.shape[0] - depth
    post(
        place_ref,
        [
            halves(first_turns),
            halves(last_turns),
            gram_halves(gram),
            halves(matmul(jnp.concatenate(sums, axis=1), rotation)),
        ],
        inner_out_ref.at[:body, :],
        outer_out_ref.at[:body, :],
    )
    is_first = place == 0
    inner_out_ref[body:, :] = jnp.where(
        is_first, onward[1], jnp.where(even, onward[0], backward[1])
    )
    outer_out_ref[body:, :] = jnp.where(
        is_first, backward[0], jnp.where(even, backward[1], onward[0])
    )

    @pl.when(is_first | (place == slots - 1))
    def _():
        outer_out_ref[:depth, :] = last_turns[:, :half]
        outer_out_ref[depth : 2 * depth, :] = first_turns[:, :half]


def third_kernel(
    floor_value,
    place_ref,
    inner_ref,
    outer_ref,
    sums_ref,
    own_ref,
    block_ref,
    before_ref,
    after_ref,
    rows_ref,
    columns_ref,
    inner_out_ref,
    outer_out_ref,
):
    even = is_even(place_ref)
    rows, columns = orderings_of(rows_ref, columns_ref)
    packed = square(own_ref, 0)
    depth = packed.shape[0]
    half = depth // 2
    upper_half = packed[:half]
    raw = jnp.concatenate(
        [
            upper_half,
            jnp.concatenate([upper_half[:, half:].T, packed[half:, half:]], axis=1),
        ],
        axis=0,
    )
    (left_a, right_a), (left_b, right_b), (gram_upper, gram_lower), sums, (onward, backward) = (
        received(even, inner_ref, outer_ref, (depth, depth, half, 8, depth))
    )
    cross = inner(
        jnp.concatenate([onward, left_a, left_b], axis=0),
        jnp.concatenate(
            [right_a, matmul(square(sums_ref, 1), right_b), matmul(raw, right_a) + backward],
            axis=0,
        ),
    )
    block = block_ref[...]
    data = jnp.concatenate(
        [
            matmul(before_ref[...], left_a) + matmul(block, left_b),
            matmul(block, right_a) + matmul(after_ref[...], right_b),
        ],
        axis=1,
    )
    rotation = solve(joined(gram_upper, gram_lower, cross), rows, columns, False)[1]
    data = matmul(data, rotation)
    totals = matmul(jnp.concatenate(sums, axis=1), rotation)[:1]
    data = data * (totals / jnp.maximum(jnp.abs(totals), floor_value))
    post(place_ref, [halves(data)], inner_out_ref, outer_out_ref)


def whole(array):
    return array, pl.BlockSpec(memory_space=pltpu.VMEM)


def after_it(array):
    return array, pl.BlockSpec(memory_space=pl.ANY)


def scalar(array):
    return array, pl.BlockSpec(memory_space=pltpu.SMEM)


def call(kernel, outs, microseconds, *operands):
    shapes = [jax.ShapeDtypeStruct(shape, F32) for shape in outs]
    vmem = pl.BlockSpec(memory_space=pltpu.VMEM)
    return pl.pallas_call(
        kernel,
        out_shape=shapes,
        in_specs=[spec for _, spec in operands],
        out_specs=[vmem] * len(shapes),
        compiler_params=pltpu.CompilerParams(vmem_limit_bytes=10 * 2**20),
        cost_estimate=pl.CostEstimate(
            flops=int(microseconds * 1e9), bytes_accessed=2**20, transcendentals=0
        ),
    )(*[array for array, _ in operands])


def reduced(parts, *first):
    (total,) = call(total_kernel, [parts.shape[1:]], 1, whole(along_ring(parts)))
    across = [(r, r ^ 1) for r in range(lax.axis_size("row"))]
    other = lax.ppermute(total, "row", across)
    (spread,) = call(spread_kernel, [parts.shape], 1, whole(total), whole(other), *first)
    return along_ring(spread)


def shards(thickness, pairing):
    cells, width = thickness.shape
    half = width // 2
    slots = lax.axis_size("col")
    position = lax.axis_index("col")
    place = scalar(jnp.full((1,), position, jnp.int32))
    floor_value = math.sqrt(float(cells * lax.axis_size("row")))
    orders = [(whole(pairing[s]), whole(pairing[s].T)) for s in range(3)]
    block = whole(thickness)
    peers = lax.axis_size("row") // 2
    chunk = width // peers
    inside, outside = chip_swap(thickness), outer_swap(thickness)
    far_before, far_after = shifted(thickness, "col", 2), shifted(thickness, "col", -2)
    (own,) = call(own_gram_kernel, [(peers, chunk, width)], 1, block)
    own = reduced(own)
    ahead, before, after = call(
        functools.partial(ahead_kernel, slots),
        [(peers, 2 * chunk, width), (cells, width), (cells, width)],
        2,
        place,
        whole(inside),
        whole(outside),
        whole(far_before),
        whole(far_after),
    )
    shape = (width + half + 8, half)
    inside, outside = call(first_kernel, [shape] * 2, 6, place, whole(own), *orders[0])
    sums = whole(reduced(ahead, after_it(inside)))
    outside, inside = outer_swap(outside), chip_swap(inside)
    shape = (3 * width + half + 8, half)
    inside, outside = call(
        functools.partial(second_kernel, slots),
        [shape] * 2,
        8,
        place,
        whole(inside),
        whole(outside),
        sums,
        *orders[1],
    )
    outside, inside = outer_swap(outside), chip_swap(inside)
    inside, outside = call(
        functools.partial(third_kernel, floor_value),
        [(cells, half)] * 2,
        8,
        place,
        whole(inside),
        whole(outside),
        sums,
        whole(own),
        block,
        whole(before),
        whole(after),
        *orders[2],
    )
    outside, inside = outer_swap(outside), chip_swap(inside)
    even = lax.rem(position, 2) == 0
    return jnp.concatenate(in_order(even, inside, outside), axis=1)


def solution(mesh):
    placed = (P("row", "col"), P())
    return jax.shard_map(
        shards, mesh=mesh, in_specs=placed, out_specs=P("row", "col"), check_vma=False
    )
```

time: 148 us -> 137 us (0.926)
  blocking collectives: 35 us -> 0 us
  starting transfers between devices: 50.6 us -> 77.7 us
  local copies, waits for them, and re-layouts: 4.87 us -> 3.03 us
  waiting for transfers between devices: 31.2 us -> 29.5 us
    ppermute x0 -> x10, starting transfers between devices: none -> 49.9 us  [the longest x4 17.1 us: outer_swap(): return lax.ppermute(array, 'col', pairs)]
    all_to_all x1 -> x0, blocking collectives: 35 us -> none  [shards(): handed = lax.all_to_all(handed, 'row', 0, 0)]
    ppermute x10 -> x2, starting transfers between devices: 29.7 us -> 5.28 us  [shifted(): return lax.ppermute(array, axis, pairs)]
    ppermute x10 -> x2, waiting for transfers between devices: 31.2 us -> 7.81 us  [shifted(): return lax.ppermute(array, axis, pairs)]
    ppermute x0 -> x10, waiting for transfers between devices: none -> 16.1 us  [the longest x4 14.6 us: outer_swap(): return lax.ppermute(array, 'col', pairs)]
    all_to_all x2 -> x4, waiting for transfers between devices: 0.01 us -> 5.54 us  [along_ring(): return lax.all_to_all(parts, 'row', 0, 0, axis_index_groups=rings)]
    unnamed x17 -> x13, local copies, waits for them, and re-layouts: 4.87 us -> 3.03 us
    all_to_all x2 -> x4, starting transfers between devices: 20.9 us -> 22.6 us  [along_ring(): return lax.all_to_all(parts, 'row', 0, 0, axis_index_groups=rings)]
  transfers between devices with their start and end apart: 12 -> 16, of which waited for: 8 -> 10; matrix products, arithmetic and copies ran while one was open for 0% -> 0% of each run, Pallas kernels for 4% -> 6%
where the time goes in v3:
time: 137 us; the launch traced here: 136 us
  starting transfers between devices  77.7 us (57%)
  waiting for transfers between devices  29.5 us (22%)
  Pallas kernels  24.4 us (18%)
  local copies, waits for them, and re-layouts  3.03 us (2%)
    pallas_call x9, Pallas kernels, call(): pl.pallas_call(kernel, out_shape=shapes, in_specs=[spec for _, spec in op...  24.4 us
    all_to_all x4, starting transfers between devices, along_ring(): return lax.all_to_all(parts, 'row', 0, 0, axis_index_groups=rings)  22.6 us
    ppermute x4, starting transfers between devices, outer_swap(): return lax.ppermute(array, 'col', pairs)  17.1 us
    ppermute x2, starting transfers between devices, reduced(): other = lax.ppermute(total, 'row', across)  16.7 us
    ppermute x4, starting transfers between devices, chip_swap(): return lax.ppermute(array, 'col', [(m, m ^ 1) for m in range(slots)])  16 us
    ppermute x4, waiting for transfers between devices, outer_swap(): return lax.ppermute(array, 'col', pairs)  14.6 us
    ppermute x2, waiting for transfers between devices, shifted(): return lax.ppermute(array, axis, pairs)  7.81 us
    all_to_all x4, waiting for transfers between devices, along_ring(): return lax.all_to_all(parts, 'row', 0, 0, axis_index_groups=rings)  5.54 us
  transfers between devices with their start and end apart: 16, of which 10 were waited for; matrix products, arithmetic and copies ran while one was open for 0% of the time, Pallas kernels for 6%

profile of v3, /device:TPU:7, one launch (start us, length us, event | category | flops | bytes accessed | tf_op | source)
XLA Modules:
  0.0 135.5 jit_solution(16204242043778416435)
XLA Ops:
  0.0 0.9 copy-done
  1.0 1.1 shard_map.28
  2.1 7.0 %all-to-all-start = ((f32[8,32,256]{2,1,0:T(8,128)}), f32[8,32,256]{2,1,0:T(8,128)S(1)}, u32[]{:S(2)}, u32[]{:S(2)}) async-start(f32[8,32,256]{2,1,0:T(8,128)} %shard_map.28), calls=%async_computation | async-start | bytes 524288 | tf_op jit(solution)/shard_map/all_to_all | solution.py:109
  9.0 2.9 %collective-permute-start.3 = (f32[256,256]{1,0:T(8,128)S(1)}, f32[256,256]{1,0:T(8,128)S(1)}, u32[]{:S(2)}, u32[]{:S(2)}) collective-permute-start(f32[256,256]{1,0:T(8,128)S(1)} %copy-done.1), channel_id=1, source_target_pairs={{0,16},{16,0},{32,48},{48,32},{64,80},{80,64},{96,112},{112,96},{1... | collective-permute-start | bytes 786440 | tf_op jit(solution)/shard_map/ppermute | solution.py:114
  11.9 3.8 %collective-permute-start.4 = (f32[256,256]{1,0:T(8,128)S(1)}, f32[256,256]{1,0:T(8,128)S(1)}, u32[]{:S(2)}, u32[]{:S(2)}) collective-permute-start(f32[256,256]{1,0:T(8,128)S(1)} %copy-done.1), channel_id=1, source_target_pairs={{0,0},{16,32},{32,16},{48,64},{64,48},{80,96},{96,80},{112,128},{1... | collective-permute-start | bytes 786440 | tf_op jit(solution)/shard_map/ppermute | solution.py:120
  15.7 3.1 %collective-permute-start.5 = (f32[256,256]{1,0:T(8,128)S(1)}, f32[256,256]{1,0:T(8,128)S(1)}, u32[]{:S(2)}, u32[]{:S(2)}) collective-permute-start(f32[256,256]{1,0:T(8,128)S(1)} %copy-done.1), channel_id=1, source_target_pairs={{0,32},{16,48},{32,64},{48,80},{64,96},{80,112},{96,128},{112,144}... | collective-permute-start | bytes 786440 | tf_op jit(solution)/shard_map/ppermute | solution.py:18
  18.9 2.2 %collective-permute-start.6 = (f32[256,256]{1,0:T(8,128)S(1)}, f32[256,256]{1,0:T(8,128)S(1)}, u32[]{:S(2)}, u32[]{:S(2)}) collective-permute-start(f32[256,256]{1,0:T(8,128)S(1)} %copy-done.1), channel_id=1, source_target_pairs={{32,0},{48,16},{64,32},{80,48},{96,64},{112,80},{128,96},{144,112}... | collective-permute-start | bytes 786440 | tf_op jit(solution)/shard_map/ppermute | solution.py:18
  21.7 3.4 %collective-permute-done.5.far_before_ref = f32[256,256]{1,0:T(8,128)S(1)} collective-permute-done((f32[256,256]{1,0:T(8,128)S(1)}, f32[256,256]{1,0:T(8,128)S(1)}, u32[]{:S(2)}, u32[]{:S(2)}) %collective-permute-start.5) | collective-permute-done | bytes 262176 | tf_op jit(solution)/shard_map/ppermute | solution.py:18
  25.2 4.4 %collective-permute-done.6.far_after_ref = f32[256,256]{1,0:T(8,128)S(1)} collective-permute-done((f32[256,256]{1,0:T(8,128)S(1)}, f32[256,256]{1,0:T(8,128)S(1)}, u32[]{:S(2)}, u32[]{:S(2)}) %collective-permute-start.6) | collective-permute-done | bytes 262176 | tf_op jit(solution)/shard_map/ppermute | solution.py:18
  29.5 1.6 %shard_map.32 = (f32[8,64,256]{2,1,0:T(8,128)}, f32[256,256]{1,0:T(8,128)S(1)}, f32[256,256]{1,0:T(8,128)S(1)}) custom-call(s32[1]{0:T(128)} %bitcast.place_ref, f32[256,256]{1,0:T(8,128)S(1)} %collective-permute-done.3.inner_ref, f32[256,256]{1,0:T(8,128)S(1)} %collective-permute-done.4.outer_ref, f32[256,256]{1,0:T(8,128)S(1)} %collective-permute-done.5.far_before_ref, ...), custom_call_target="tpu_custom_call" | custom-call | flops 2000000000 | bytes 1048576 | tf_op jit(solution)/shard_map/pallas_call | solution.py:382
  31.8 6.9 %all-to-all-start.2 = ((f32[8,64,256]{2,1,0:T(8,128)}), f32[8,64,256]{2,1,0:T(8,128)S(1)}, u32[]{:S(2)}, u32[]{:S(2)}) async-start(f32[8,64,256]{2,1,0:T(8,128)} %get-tuple-element.16), calls=%async_computation.2 | async-start | bytes 1048576 | tf_op jit(solution)/shard_map/all_to_all | solution.py:109
  38.8 8.8 %collective-permute-start = (f32[32,256]{1,0:T(8,128)S(1)}, f32[32,256]{1,0:T(8,128)S(1)}, u32[]{:S(2)}, u32[]{:S(2)}) collective-permute-start(f32[32,256]{1,0:T(8,128)S(1)} %shard_map.29.one_ref), channel_id=1, source_target_pairs={{0,1},{1,0},{2,3},{3,2},{4,5},{5,4},{6,7},{7,6},{8,9},{9,8},{10,11... | collective-permute-start | bytes 98312 | tf_op jit(solution)/shard_map/ppermute | solution.py:397
  47.6 1.3 collective-permute-done.other_ref
  49.6 4.3 %all-to-all-done.2.in_ref = f32[8,64,256]{2,1,0:T(8,128)S(1)} async-done(((f32[8,64,256]{2,1,0:T(8,128)}), f32[8,64,256]{2,1,0:T(8,128)S(1)}, u32[]{:S(2)}, u32[]{:S(2)}) %all-to-all-start.2) | async-done | bytes 524320 | tf_op jit(solution)/shard_map/all_to_all | solution.py:109
  53.9 3.4 %all-to-all-start.1 = ((f32[8,32,256]{2,1,0:T(8,128)}), f32[8,32,256]{2,1,0:T(8,128)S(1)}, u32[]{:S(2)}, u32[]{:S(2)}) async-start(f32[8,32,256]{2,1,0:T(8,128)} %shard_map.30), calls=%async_computation.1 | async-start | bytes 524288 | tf_op jit(solution)/shard_map/all_to_all | solution.py:109
  57.5 7.9 %collective-permute-start.7 = (f32[64,256]{1,0:T(8,128)S(1)}, f32[64,256]{1,0:T(8,128)S(1)}, u32[]{:S(2)}, u32[]{:S(2)}) collective-permute-start(f32[64,256]{1,0:T(8,128)S(1)} %shard_map.33.one_ref), channel_id=1, source_target_pairs={{0,1},{1,0},{2,3},{3,2},{4,5},{5,4},{6,7},{7,6},{8,9},{9,8},{10,11... | collective-permute-start | bytes 196616 | tf_op jit(solution)/shard_map/ppermute | solution.py:397
  65.4 1.3 all-to-all-done.1.sums_ref.own_ref
  66.7 5.6 %shard_map.31 = (f32[392,128]{1,0:T(8,128)S(1)}, f32[392,128]{1,0:T(8,128)S(1)}) custom-call(s32[1]{0:T(128)} %bitcast.place_ref, f32[8,32,256]{2,1,0:T(8,128)S(1)} %all-to-all-done.1.sums_ref.own_ref, s32[6,256]{1,0:T(8,128)S(1)} %get-tuple-element.26.rows_ref, s32[256,6]{1,0:T(8,128)S(1)} %bitcast.18), custom_call_target="tpu_custom_call" | custom-call | flops 6000000000 | bytes 1048576 | tf_op jit(solution)/shard_map/pallas_call | solution.py:382
  72.3 0.9 shard_map.34
  73.2 5.3 %all-to-all-start.3 = ((f32[8,64,256]{2,1,0:T(8,128)}), f32[8,64,256]{2,1,0:T(8,128)S(1)}, u32[]{:S(2)}, u32[]{:S(2)}) async-start(f32[8,64,256]{2,1,0:T(8,128)} %shard_map.34), calls=%async_computation.3 | async-start | bytes 1048576 | tf_op jit(solution)/shard_map/all_to_all | solution.py:109
  78.5 7.0 %collective-permute-start.1 = (f32[392,128]{1,0:T(8,128)S(1)}, f32[392,128]{1,0:T(8,128)S(1)}, u32[]{:S(2)}, u32[]{:S(2)}) collective-permute-start(f32[392,128]{1,0:T(8,128)S(1)} %get-tuple-element.14.refs_0_), channel_id=1, source_target_pairs={{0,16},{16,0},{32,48},{48,32},{64,80},{80,64},{96,112},{112,96},{1... | collective-permute-start | bytes 602120 | tf_op jit(solution)/shard_map/ppermute | solution.py:114
  85.5 2.6 %collective-permute-start.2 = (f32[392,128]{1,0:T(8,128)S(1)}, f32[392,128]{1,0:T(8,128)S(1)}, u32[]{:S(2)}, u32[]{:S(2)}) collective-permute-start(f32[392,128]{1,0:T(8,128)S(1)} %get-tuple-element.15), channel_id=1, source_target_pairs={{0,0},{16,32},{32,16},{48,64},{64,48},{80,96},{96,80},{112,128},{1... | collective-permute-start | bytes 602120 | tf_op jit(solution)/shard_map/ppermute | solution.py:120
  88.3 6.4 %collective-permute-done.2.outer_ref = f32[392,128]{1,0:T(8,128)S(1)} collective-permute-done((f32[392,128]{1,0:T(8,128)S(1)}, f32[392,128]{1,0:T(8,128)S(1)}, u32[]{:S(2)}, u32[]{:S(2)}) %collective-permute-start.2) | collective-permute-done | bytes 200736 | tf_op jit(solution)/shard_map/ppermute | solution.py:120
  94.6 7.2 %shard_map.35 = (f32[904,128]{1,0:T(8,128)S(1)}, f32[904,128]{1,0:T(8,128)S(1)}) custom-call(s32[1]{0:T(128)} %bitcast.place_ref, f32[392,128]{1,0:T(8,128)S(1)} %collective-permute-done.1.inner_ref, f32[392,128]{1,0:T(8,128)S(1)} %collective-permute-done.2.outer_ref, f32[8,64,256]{2,1,0:T(8,128)S(1)} %all-to-all-done.3.sums_ref, ...), custom_call_target="tpu_custom_call" | custom-call | flops 8000000000 | bytes 1048576 | tf_op jit(solution)/shard_map/pallas_call | solution.py:382
  101.9 4.3 %collective-permute-start.8 = (f32[904,128]{1,0:T(8,128)S(1)}, f32[904,128]{1,0:T(8,128)S(1)}, u32[]{:S(2)}, u32[]{:S(2)}) collective-permute-start(f32[904,128]{1,0:T(8,128)S(1)} %get-tuple-element.17), channel_id=1, source_target_pairs={{0,16},{16,0},{32,48},{48,32},{64,80},{80,64},{96,112},{112,96},{1... | collective-permute-start | bytes 1388552 | tf_op jit(solution)/shard_map/ppermute | solution.py:114
  106.1 5.3 %collective-permute-start.9 = (f32[904,128]{1,0:T(8,128)S(1)}, f32[904,128]{1,0:T(8,128)S(1)}, u32[]{:S(2)}, u32[]{:S(2)}) collective-permute-start(f32[904,128]{1,0:T(8,128)S(1)} %get-tuple-element.18), channel_id=1, source_target_pairs={{0,0},{16,32},{32,16},{48,64},{64,48},{80,96},{96,80},{112,128},{1... | collective-permute-start | bytes 1388552 | tf_op jit(solution)/shard_map/ppermute | solution.py:120
  111.6 6.5 %collective-permute-done.9.outer_ref = f32[904,128]{1,0:T(8,128)S(1)} collective-permute-done((f32[904,128]{1,0:T(8,128)S(1)}, f32[904,128]{1,0:T(8,128)S(1)}, u32[]{:S(2)}, u32[]{:S(2)}) %collective-permute-start.9) | collective-permute-done | bytes 462880 | tf_op jit(solution)/shard_map/ppermute | solution.py:120
  118.1 0.9 copy-done.3
  119.0 7.2 %shard_map.36 = (f32[256,128]{1,0:T(8,128)S(1)}, f32[256,128]{1,0:T(8,128)S(1)}) custom-call(s32[1]{0:T(128)} %bitcast.place_ref, f32[904,128]{1,0:T(8,128)S(1)} %collective-permute-done.8.inner_ref, f32[904,128]{1,0:T(8,128)S(1)} %collective-permute-done.9.outer_ref, f32[8,64,256]{2,1,0:T(8,128)S(1)} %all-to-all-done.3.sums_ref, ...), custom_call_target="tpu_custom_call" | custom-call | flops 8000000000 | bytes 1048576 | tf_op jit(solution)/shard_map/pallas_call | solution.py:382
  126.2 5.3 %collective-permute-start.10 = (f32[256,128]{1,0:T(8,128)S(1)}, f32[256,128]{1,0:T(8,128)S(1)}, u32[]{:S(2)}, u32[]{:S(2)}) collective-permute-start(f32[256,128]{1,0:T(8,128)S(1)} %get-tuple-element.21), channel_id=1, source_target_pairs={{0,0},{16,32},{32,16},{48,64},{64,48},{80,96},{96,80},{112,128},{1... | collective-permute-start | bytes 393224 | tf_op jit(solution)/shard_map/ppermute | solution.py:120
  131.5 1.9 %collective-permute-start.11 = (f32[256,128]{1,0:T(8,128)S(1)}, f32[256,128]{1,0:T(8,128)S(1)}, u32[]{:S(2)}, u32[]{:S(2)}) collective-permute-start(f32[256,128]{1,0:T(8,128)S(1)} %get-tuple-element.22), channel_id=1, source_target_pairs={{0,16},{16,0},{32,48},{48,32},{64,80},{80,64},{96,112},{112,96},{1... | collective-permute-start | bytes 393224 | tf_op jit(solution)/shard_map/ppermute | solution.py:114
  133.5 1.1 collective-permute-done.10
  (25 shorter events, 3.5 us)
Async XLA Ops:
  0.0 0.9 copy-start
  2.1 7.0 %copy-start.1 = (f32[256,256]{1,0:T(8,128)S(1)}, f32[256,256]{1,0:T(8,128)}, u32[]{:S(2)}) copy-start(f32[256,256]{1,0:T(8,128)} %block_ref.3) | copy-start | bytes 786436
  2.1 29.7 %all-to-all-start = ((f32[8,32,256]{2,1,0:T(8,128)}), f32[8,32,256]{2,1,0:T(8,128)S(1)}, u32[]{:S(2)}, u32[]{:S(2)}) async-start(f32[8,32,256]{2,1,0:T(8,128)} %shard_map.28), calls=%async_computation | async-start | bytes 524288 | tf_op jit(solution)/shard_map/all_to_all | solution.py:109
  9.0 12.0 %collective-permute-start.3 = (f32[256,256]{1,0:T(8,128)S(1)}, f32[256,256]{1,0:T(8,128)S(1)}, u32[]{:S(2)}, u32[]{:S(2)}) collective-permute-start(f32[256,256]{1,0:T(8,128)S(1)} %copy-done.1), channel_id=1, source_target_pairs={{0,16},{16,0},{32,48},{48,32},{64,80},{80,64},{96,112},{112,96},{1... | collective-permute-start | bytes 786440 | tf_op jit(solution)/shard_map/ppermute | solution.py:114
  11.9 9.8 %collective-permute-start.4 = (f32[256,256]{1,0:T(8,128)S(1)}, f32[256,256]{1,0:T(8,128)S(1)}, u32[]{:S(2)}, u32[]{:S(2)}) collective-permute-start(f32[256,256]{1,0:T(8,128)S(1)} %copy-done.1), channel_id=1, source_target_pairs={{0,0},{16,32},{32,16},{48,64},{64,48},{80,96},{96,80},{112,128},{1... | collective-permute-start | bytes 786440 | tf_op jit(solution)/shard_map/ppermute | solution.py:120
  15.7 9.4 %collective-permute-start.5 = (f32[256,256]{1,0:T(8,128)S(1)}, f32[256,256]{1,0:T(8,128)S(1)}, u32[]{:S(2)}, u32[]{:S(2)}) collective-permute-start(f32[256,256]{1,0:T(8,128)S(1)} %copy-done.1), channel_id=1, source_target_pairs={{0,32},{16,48},{32,64},{48,80},{64,96},{80,112},{96,128},{112,144}... | collective-permute-start | bytes 786440 | tf_op jit(solution)/shard_map/ppermute | solution.py:18
  18.9 10.7 %collective-permute-start.6 = (f32[256,256]{1,0:T(8,128)S(1)}, f32[256,256]{1,0:T(8,128)S(1)}, u32[]{:S(2)}, u32[]{:S(2)}) collective-permute-start(f32[256,256]{1,0:T(8,128)S(1)} %copy-done.1), channel_id=1, source_target_pairs={{32,0},{48,16},{64,32},{80,48},{96,64},{112,80},{128,96},{144,112}... | collective-permute-start | bytes 786440 | tf_op jit(solution)/shard_map/ppermute | solution.py:18
  31.1 0.7 copy-start.2
  31.8 22.1 %all-to-all-start.2 = ((f32[8,64,256]{2,1,0:T(8,128)}), f32[8,64,256]{2,1,0:T(8,128)S(1)}, u32[]{:S(2)}, u32[]{:S(2)}) async-start(f32[8,64,256]{2,1,0:T(8,128)} %get-tuple-element.16), calls=%async_computation.2 | async-start | bytes 1048576 | tf_op jit(solution)/shard_map/all_to_all | solution.py:109
  38.8 10.1 %collective-permute-start = (f32[32,256]{1,0:T(8,128)S(1)}, f32[32,256]{1,0:T(8,128)S(1)}, u32[]{:S(2)}, u32[]{:S(2)}) collective-permute-start(f32[32,256]{1,0:T(8,128)S(1)} %shard_map.29.one_ref), channel_id=1, source_target_pairs={{0,1},{1,0},{2,3},{3,2},{4,5},{5,4},{6,7},{7,6},{8,9},{9,8},{10,11... | collective-permute-start | bytes 98312 | tf_op jit(solution)/shard_map/ppermute | solution.py:397
  49.6 7.7 %copy-start.4 = (s32[3,6,256]{2,1,0:T(8,128)S(1)}, s32[3,6,256]{2,1,0:T(8,128)}, u32[]{:S(2)}) copy-start(s32[3,6,256]{2,1,0:T(8,128)} %param.3) | copy-start | bytes 55300
  53.9 12.8 %all-to-all-start.1 = ((f32[8,32,256]{2,1,0:T(8,128)}), f32[8,32,256]{2,1,0:T(8,128)S(1)}, u32[]{:S(2)}, u32[]{:S(2)}) async-start(f32[8,32,256]{2,1,0:T(8,128)} %shard_map.30), calls=%async_computation.1 | async-start | bytes 524288 | tf_op jit(solution)/shard_map/all_to_all | solution.py:109
  57.5 14.8 %collective-permute-start.7 = (f32[64,256]{1,0:T(8,128)S(1)}, f32[64,256]{1,0:T(8,128)S(1)}, u32[]{:S(2)}, u32[]{:S(2)}) collective-permute-start(f32[64,256]{1,0:T(8,128)S(1)} %shard_map.33.one_ref), channel_id=1, source_target_pairs={{0,1},{1,0},{2,3},{3,2},{4,5},{5,4},{6,7},{7,6},{8,9},{9,8},{10,11... | collective-permute-start | bytes 196616 | tf_op jit(solution)/shard_map/ppermute | solution.py:397
  73.2 21.4 %all-to-all-start.3 = ((f32[8,64,256]{2,1,0:T(8,128)}), f32[8,64,256]{2,1,0:T(8,128)S(1)}, u32[]{:S(2)}, u32[]{:S(2)}) async-start(f32[8,64,256]{2,1,0:T(8,128)} %shard_map.34), calls=%async_computation.3 | async-start | bytes 1048576 | tf_op jit(solution)/shard_map/all_to_all | solution.py:109
  78.5 9.8 %collective-permute-start.1 = (f32[392,128]{1,0:T(8,128)S(1)}, f32[392,128]{1,0:T(8,128)S(1)}, u32[]{:S(2)}, u32[]{:S(2)}) collective-permute-start(f32[392,128]{1,0:T(8,128)S(1)} %get-tuple-element.14.refs_0_), channel_id=1, source_target_pairs={{0,16},{16,0},{32,48},{48,32},{64,80},{80,64},{96,112},{112,96},{1... | collective-permute-start | bytes 602120 | tf_op jit(solution)/shard_map/ppermute | solution.py:114
  85.5 9.1 %collective-permute-start.2 = (f32[392,128]{1,0:T(8,128)S(1)}, f32[392,128]{1,0:T(8,128)S(1)}, u32[]{:S(2)}, u32[]{:S(2)}) collective-permute-start(f32[392,128]{1,0:T(8,128)S(1)} %get-tuple-element.15), channel_id=1, source_target_pairs={{0,0},{16,32},{32,16},{48,64},{64,48},{80,96},{96,80},{112,128},{1... | collective-permute-start | bytes 602120 | tf_op jit(solution)/shard_map/ppermute | solution.py:120
  101.9 9.7 %collective-permute-start.8 = (f32[904,128]{1,0:T(8,128)S(1)}, f32[904,128]{1,0:T(8,128)S(1)}, u32[]{:S(2)}, u32[]{:S(2)}) collective-permute-start(f32[904,128]{1,0:T(8,128)S(1)} %get-tuple-element.17), channel_id=1, source_target_pairs={{0,16},{16,0},{32,48},{48,32},{64,80},{80,64},{96,112},{112,96},{1... | collective-permute-start | bytes 1388552 | tf_op jit(solution)/shard_map/ppermute | solution.py:114
  106.1 12.0 %collective-permute-start.9 = (f32[904,128]{1,0:T(8,128)S(1)}, f32[904,128]{1,0:T(8,128)S(1)}, u32[]{:S(2)}, u32[]{:S(2)}) collective-permute-start(f32[904,128]{1,0:T(8,128)S(1)} %get-tuple-element.18), channel_id=1, source_target_pairs={{0,0},{16,32},{32,16},{48,64},{64,48},{80,96},{96,80},{112,128},{1... | collective-permute-start | bytes 1388552 | tf_op jit(solution)/shard_map/ppermute | solution.py:120
  118.1 1.0 copy-start.3
  126.2 8.4 %collective-permute-start.10 = (f32[256,128]{1,0:T(8,128)S(1)}, f32[256,128]{1,0:T(8,128)S(1)}, u32[]{:S(2)}, u32[]{:S(2)}) collective-permute-start(f32[256,128]{1,0:T(8,128)S(1)} %get-tuple-element.21), channel_id=1, source_target_pairs={{0,0},{16,32},{32,16},{48,64},{64,48},{80,96},{96,80},{112,128},{1... | collective-permute-start | bytes 393224 | tf_op jit(solution)/shard_map/ppermute | solution.py:120
  131.5 3.2 %collective-permute-start.11 = (f32[256,128]{1,0:T(8,128)S(1)}, f32[256,128]{1,0:T(8,128)S(1)}, u32[]{:S(2)}, u32[]{:S(2)}) collective-permute-start(f32[256,128]{1,0:T(8,128)S(1)} %get-tuple-element.22), channel_id=1, source_target_pairs={{0,16},{16,0},{32,48},{48,32},{64,80},{80,64},{96,112},{112,96},{1... | collective-permute-start | bytes 393224 | tf_op jit(solution)/shard_map/ppermute | solution.py:114

commit v4 on v3

--- a/solution.py
+++ b/solution.py
@@ -169,10 +169,10 @@
 def ahead_kernel(
     slots,
     place_ref,
+    outer_ref,
     inner_ref,
-    outer_ref,
+    far_after_ref,
     far_before_ref,
-    far_after_ref,
     out_ref,
     before_ref,
     after_ref,
@@ -223,7 +223,9 @@
     return gram[:half, :half], gram[half:, half:]
 
 
-def first_kernel(place_ref, sums_ref, rows_ref, columns_ref, *outs):
+def first_kernel(
+    place_ref, sums_ref, block_ref, rows_ref, columns_ref, inner_out_ref, outer_out_ref, data_ref, pair_ref
+):
     rows, columns = orderings_of(rows_ref, columns_ref)
     packed = square(sums_ref, 0)
     half = packed.shape[1] // 2
@@ -237,11 +239,18 @@
     sums = jnp.concatenate([packed[half : half + 1, :half], packed[half + 1 : half + 2, :half]], 1)
     sums = jnp.broadcast_to(sums, (8, 2 * half))
     gram, rotation = solve(gram, rows, columns, True)
+    upper, lower = halves(rotation)
     post(
         place_ref,
-        [halves(rotation), gram_halves(gram), halves(matmul(sums, rotation))],
-        *outs,
-    )
+        [(upper, lower), (lower, upper), gram_halves(gram), halves(matmul(sums, rotation))],
+        inner_out_ref,
+        outer_out_ref,
+    )
+    is_first = place_ref[0] == 0
+    data = matmul(block_ref[...], rotation)
+    data_ref[:, :half] = jnp.where(is_first, data[:, half:], data[:, :half])
+    data_ref[:, half:] = jnp.where(is_first, data[:, :half], data[:, half:])
+    pair_ref[...] = jnp.where(is_first, gram[:half, half:], gram[half:, :half])
 
 
 def received(even, inner_ref, outer_ref, sizes):
@@ -265,60 +274,52 @@
 
 
 def second_kernel(
-    slots, place_ref, inner_ref, outer_ref, sums_ref, rows_ref, columns_ref, *outs
+    place_ref, inner_ref, outer_ref, sums_ref, rows_ref, columns_ref, *outs
 ):
-    place = place_ref[0]
     even = is_even(place_ref)
     rows, columns = orderings_of(rows_ref, columns_ref)
     near = square(sums_ref, 0)
     depth = near.shape[0]
     half = depth // 2
-    (turn_upper, turn_lower), (gram_upper, gram_lower), sums = received(
-        even, inner_ref, outer_ref, (depth, half, 8)
-    )
-    onward, backward = inner(near, turn_upper), matmul(near, turn_lower)
+    (turn_upper, turn_lower), (other_upper, other_lower), (gram_upper, gram_lower), sums = (
+        received(even, inner_ref, outer_ref, (depth, depth, half, 8))
+    )
+    backward = matmul(near, turn_lower)
     cross = inner(turn_upper, backward)
-    first = jnp.concatenate([turn_upper, onward], axis=0)
-    last = jnp.concatenate([turn_lower, backward], axis=0)
+    onward = jnp.concatenate(
+        [turn_upper, inner(matmul(near, other_lower), turn_upper)], axis=0
+    )
+    backward = jnp.concatenate([turn_lower, inner(other_upper, backward)], axis=0)
     gram, rotation = solve(joined(gram_upper, gram_lower, cross), rows, columns, True)
-    first, last = matmul(first, rotation[:half]), matmul(last, rotation[half:])
-    first_turns, last_turns = first[:depth], last[:depth]
-    onward, backward = halves(first[depth:]), halves(last[depth:])
+    onward, backward = matmul(onward, rotation[:half]), matmul(backward, rotation[half:])
+    onward = jnp.concatenate([onward, rotation[half:]], axis=0)
+    backward = jnp.concatenate([backward, rotation[:half]], axis=0)
     inner_out_ref, outer_out_ref = outs
-    body = inner_out_ref.shape[0] - depth
+    body = 2 * depth
     post(
         place_ref,
-        [
-            halves(first_turns),
-            halves(last_turns),
-            gram_halves(gram),
-            halves(matmul(jnp.concatenate(sums, axis=1), rotation)),
-        ],
-        inner_out_ref.at[:body, :],
-        outer_out_ref.at[:body, :],
-    )
-    is_first = place == 0
-    inner_out_ref[body:, :] = jnp.where(
+        [gram_halves(gram), halves(matmul(jnp.concatenate(sums, axis=1), rotation))],
+        inner_out_ref.at[body:, :],
+        outer_out_ref.at[body:, :],
+    )
+    is_first = place_ref[0] == 0
+    onward, backward = halves(onward), halves(backward)
+    inner_out_ref[:body, :] = jnp.where(
         is_first, onward[1], jnp.where(even, onward[0], backward[1])
     )
-    outer_out_ref[body:, :] = jnp.where(
+    outer_out_ref[:body, :] = jnp.where(
         is_first, backward[0], jnp.where(even, backward[1], onward[0])
     )
-
-    @pl.when(is_first | (place == slots - 1))
-    def _():
-        outer_out_ref[:depth, :] = last_turns[:, :half]
-        outer_out_ref[depth : 2 * depth, :] = first_turns[:, :half]
 
 
 def third_kernel(
     floor_value,
     place_ref,
+    outer_ref,
     inner_ref,
-    outer_ref,
     sums_ref,
-    own_ref,
-    block_ref,
+    data_ref,
+    pair_ref,
     before_ref,
     after_ref,
     rows_ref,
@@ -328,32 +329,29 @@
 ):
     even = is_even(place_ref)
     rows, columns = orderings_of(rows_ref, columns_ref)
-    packed = square(own_ref, 0)
-    depth = packed.shape[0]
-    half = depth // 2
-    upper_half = packed[:half]
-    raw = jnp.concatenate(
-        [
-            upper_half,
-            jnp.concatenate([upper_half[:, half:].T, packed[half:, half:]], axis=1),
-        ],
-        axis=0,
-    )
-    (left_a, right_a), (left_b, right_b), (gram_upper, gram_lower), sums, (onward, backward) = (
-        received(even, inner_ref, outer_ref, (depth, depth, half, 8, depth))
-    )
+    half = pair_ref.shape[0]
+    (
+        (left_far, right_far),
+        (onward, backward),
+        (left_near, right_near),
+        (gram_upper, gram_lower),
+        sums,
+    ) = received(even, inner_ref, outer_ref, (2 * half, half, half, half, 8))
     cross = inner(
-        jnp.concatenate([onward, left_a, left_b], axis=0),
+        jnp.concatenate([onward, left_far, left_near], axis=0),
         jnp.concatenate(
-            [right_a, matmul(square(sums_ref, 1), right_b), matmul(raw, right_a) + backward],
+            [
+                right_near,
+                matmul(square(sums_ref, 1), right_far),
+                matmul(pair_ref[...], right_near) + backward,
+            ],
             axis=0,
         ),
     )
-    block = block_ref[...]
     data = jnp.concatenate(
         [
-            matmul(before_ref[...], left_a) + matmul(block, left_b),
-            matmul(block, right_a) + matmul(after_ref[...], right_b),
+            matmul(before_ref[...], left_far) + matmul(data_ref[:, half:], left_near),
+            matmul(data_ref[:, :half], right_near) + matmul(after_ref[...], right_far),
         ],
         axis=1,
     )
@@ -419,18 +417,25 @@
         [(peers, 2 * chunk, width), (cells, width), (cells, width)],
         2,
         place,
+        whole(outside),
         whole(inside),
-        whole(outside),
+        whole(far_after),
         whole(far_before),
-        whole(far_after),
-    )
-    shape = (width + half + 8, half)
-    inside, outside = call(first_kernel, [shape] * 2, 6, place, whole(own), *orders[0])
+    )
+    shape = (2 * width + half + 8, half)
+    inside, outside, data, pair = call(
+        first_kernel,
+        [shape, shape, (cells, width), (half, half)],
+        6,
+        place,
+        whole(own),
+        block,
+        *orders[0],
+    )
     sums = whole(reduced(ahead, after_it(inside)))
     outside, inside = outer_swap(outside), chip_swap(inside)
-    shape = (3 * width + half + 8, half)
     inside, outside = call(
-        functools.partial(second_kernel, slots),
+        second_kernel,
         [shape] * 2,
         8,
         place,
@@ -445,11 +450,11 @@
         [(cells, half)] * 2,
         8,
         place,
+        whole(outside),
         whole(inside),
-        whole(outside),
         sums,
-        whole(own),
-        block,
+        whole(data),
+        whole(pair),
         whole(before),
         whole(after),
         *orders[2],

time: 137 us -> 134 us (0.978)
  waiting for transfers between devices: 29.5 us -> 22.2 us
  starting transfers between devices: 77.7 us -> 81.7 us
    ppermute x4, starting transfers between devices: 17.1 us -> 28.3 us  [outer_swap(): return lax.ppermute(array, 'col', pairs)]
    ppermute x4, waiting for transfers between devices: 14.6 us -> 6.92 us  [outer_swap(): return lax.ppermute(array, 'col', pairs)]
    ppermute x4, starting transfers between devices: 16 us -> 8.81 us  [chip_swap(): return lax.ppermute(array, 'col', [(m, m ^ 1) for m in range(slots)])]
where the time goes in v4:
time: 134 us; the launch traced here: 132 us
  starting transfers between devices  81.7 us (61%)
  Pallas kernels  24.2 us (18%)
  waiting for transfers between devices  22.2 us (17%)
  local copies, waits for them, and re-layouts  3.01 us (2%)
    ppermute x4, starting transfers between devices, outer_swap(): return lax.ppermute(array, 'col', pairs)  28.3 us
    pallas_call x9, Pallas kernels, call(): pl.pallas_call(kernel, out_shape=shapes, in_specs=[spec for _, spec in op...  24.2 us
    all_to_all x4, starting transfers between devices, along_ring(): return lax.all_to_all(parts, 'row', 0, 0, axis_index_groups=rings)  22.6 us
    ppermute x2, starting transfers between devices, reduced(): other = lax.ppermute(total, 'row', across)  16.7 us
    ppermute x4, starting transfers between devices, chip_swap(): return lax.ppermute(array, 'col', [(m, m ^ 1) for m in range(slots)])  8.81 us
    ppermute x2, waiting for transfers between devices, shifted(): return lax.ppermute(array, axis, pairs)  7.81 us
    ppermute x4, waiting for transfers between devices, outer_swap(): return lax.ppermute(array, 'col', pairs)  6.92 us
    all_to_all x4, waiting for transfers between devices, along_ring(): return lax.all_to_all(parts, 'row', 0, 0, axis_index_groups=rings)  5.54 us
  transfers between devices with their start and end apart: 16, of which 10 were waited for; matrix products, arithmetic and copies ran while one was open for 0% of the time, Pallas kernels for 6%

profile of v4, /device:TPU:7, one launch (start us, length us, event | category | flops | bytes accessed | tf_op | source)
XLA Modules:
  0.0 132.1 jit_solution(10144510597253415680)
XLA Ops:
  0.0 0.9 copy-done
  1.0 1.1 shard_map.28
  2.1 7.0 %all-to-all-start = ((f32[8,32,256]{2,1,0:T(8,128)}), f32[8,32,256]{2,1,0:T(8,128)S(1)}, u32[]{:S(2)}, u32[]{:S(2)}) async-start(f32[8,32,256]{2,1,0:T(8,128)} %shard_map.28), calls=%async_computation | async-start | bytes 524288 | tf_op jit(solution)/shard_map/all_to_all | solution.py:109
  9.0 2.9 %collective-permute-start.4 = (f32[256,256]{1,0:T(8,128)S(1)}, f32[256,256]{1,0:T(8,128)S(1)}, u32[]{:S(2)}, u32[]{:S(2)}) collective-permute-start(f32[256,256]{1,0:T(8,128)S(1)} %copy-done.1), channel_id=1, source_target_pairs={{0,16},{16,0},{32,48},{48,32},{64,80},{80,64},{96,112},{112,96},{1... | collective-permute-start | bytes 786440 | tf_op jit(solution)/shard_map/ppermute | solution.py:114
  11.9 3.8 %collective-permute-start.3 = (f32[256,256]{1,0:T(8,128)S(1)}, f32[256,256]{1,0:T(8,128)S(1)}, u32[]{:S(2)}, u32[]{:S(2)}) collective-permute-start(f32[256,256]{1,0:T(8,128)S(1)} %copy-done.1), channel_id=1, source_target_pairs={{0,0},{16,32},{32,16},{48,64},{64,48},{80,96},{96,80},{112,128},{1... | collective-permute-start | bytes 786440 | tf_op jit(solution)/shard_map/ppermute | solution.py:120
  15.7 3.1 %collective-permute-start.6 = (f32[256,256]{1,0:T(8,128)S(1)}, f32[256,256]{1,0:T(8,128)S(1)}, u32[]{:S(2)}, u32[]{:S(2)}) collective-permute-start(f32[256,256]{1,0:T(8,128)S(1)} %copy-done.1), channel_id=1, source_target_pairs={{0,32},{16,48},{32,64},{48,80},{64,96},{80,112},{96,128},{112,144}... | collective-permute-start | bytes 786440 | tf_op jit(solution)/shard_map/ppermute | solution.py:18
  18.9 2.2 %collective-permute-start.5 = (f32[256,256]{1,0:T(8,128)S(1)}, f32[256,256]{1,0:T(8,128)S(1)}, u32[]{:S(2)}, u32[]{:S(2)}) collective-permute-start(f32[256,256]{1,0:T(8,128)S(1)} %copy-done.1), channel_id=1, source_target_pairs={{32,0},{48,16},{64,32},{80,48},{96,64},{112,80},{128,96},{144,112}... | collective-permute-start | bytes 786440 | tf_op jit(solution)/shard_map/ppermute | solution.py:18
  21.7 3.4 %collective-permute-done.6.far_before_ref = f32[256,256]{1,0:T(8,128)S(1)} collective-permute-done((f32[256,256]{1,0:T(8,128)S(1)}, f32[256,256]{1,0:T(8,128)S(1)}, u32[]{:S(2)}, u32[]{:S(2)}) %collective-permute-start.6) | collective-permute-done | bytes 262176 | tf_op jit(solution)/shard_map/ppermute | solution.py:18
  25.2 4.4 %collective-permute-done.5.far_after_ref = f32[256,256]{1,0:T(8,128)S(1)} collective-permute-done((f32[256,256]{1,0:T(8,128)S(1)}, f32[256,256]{1,0:T(8,128)S(1)}, u32[]{:S(2)}, u32[]{:S(2)}) %collective-permute-start.5) | collective-permute-done | bytes 262176 | tf_op jit(solution)/shard_map/ppermute | solution.py:18
  29.5 1.6 %shard_map.32 = (f32[8,64,256]{2,1,0:T(8,128)}, f32[256,256]{1,0:T(8,128)S(1)}, f32[256,256]{1,0:T(8,128)S(1)}) custom-call(s32[1]{0:T(128)} %bitcast.place_ref, f32[256,256]{1,0:T(8,128)S(1)} %collective-permute-done.3.outer_ref, f32[256,256]{1,0:T(8,128)S(1)} %collective-permute-done.4.inner_ref, f32[256,256]{1,0:T(8,128)S(1)} %collective-permute-done.5.far_after_ref, ...), custom_call_target="tpu_custom_call" | custom-call | flops 2000000000 | bytes 1048576 | tf_op jit(solution)/shard_map/pallas_call | solution.py:380
  31.1 6.9 %all-to-all-start.2 = ((f32[8,64,256]{2,1,0:T(8,128)}), f32[8,64,256]{2,1,0:T(8,128)S(1)}, u32[]{:S(2)}, u32[]{:S(2)}) async-start(f32[8,64,256]{2,1,0:T(8,128)} %get-tuple-element.18), calls=%async_computation.2 | async-start | bytes 1048576 | tf_op jit(solution)/shard_map/all_to_all | solution.py:109
  38.0 8.8 %collective-permute-start = (f32[32,256]{1,0:T(8,128)S(1)}, f32[32,256]{1,0:T(8,128)S(1)}, u32[]{:S(2)}, u32[]{:S(2)}) collective-permute-start(f32[32,256]{1,0:T(8,128)S(1)} %shard_map.29.one_ref), channel_id=1, source_target_pairs={{0,1},{1,0},{2,3},{3,2},{4,5},{5,4},{6,7},{7,6},{8,9},{9,8},{10,11... | collective-permute-start | bytes 98312 | tf_op jit(solution)/shard_map/ppermute | solution.py:395
  46.9 1.3 collective-permute-done.other_ref
  48.2 0.7 shard_map.30
  48.9 4.3 %all-to-all-done.2.in_ref = f32[8,64,256]{2,1,0:T(8,128)S(1)} async-done(((f32[8,64,256]{2,1,0:T(8,128)}), f32[8,64,256]{2,1,0:T(8,128)S(1)}, u32[]{:S(2)}, u32[]{:S(2)}) %all-to-all-start.2) | async-done | bytes 524320 | tf_op jit(solution)/shard_map/all_to_all | solution.py:109
  53.2 3.4 %all-to-all-start.1 = ((f32[8,32,256]{2,1,0:T(8,128)}), f32[8,32,256]{2,1,0:T(8,128)S(1)}, u32[]{:S(2)}, u32[]{:S(2)}) async-start(f32[8,32,256]{2,1,0:T(8,128)} %shard_map.30), calls=%async_computation.1 | async-start | bytes 524288 | tf_op jit(solution)/shard_map/all_to_all | solution.py:109
  56.8 7.9 %collective-permute-start.7 = (f32[64,256]{1,0:T(8,128)S(1)}, f32[64,256]{1,0:T(8,128)S(1)}, u32[]{:S(2)}, u32[]{:S(2)}) collective-permute-start(f32[64,256]{1,0:T(8,128)S(1)} %shard_map.33.one_ref), channel_id=1, source_target_pairs={{0,1},{1,0},{2,3},{3,2},{4,5},{5,4},{6,7},{7,6},{8,9},{9,8},{10,11... | collective-permute-start | bytes 196616 | tf_op jit(solution)/shard_map/ppermute | solution.py:395
  64.7 1.3 all-to-all-done.1.sums_ref
  66.0 5.8 %shard_map.31 = (f32[648,128]{1,0:T(8,128)S(1)}, f32[648,128]{1,0:T(8,128)S(1)}, f32[256,256]{1,0:T(8,128)S(1)}, f32[128,128]{1,0:T(8,128)S(1)}) custom-call(s32[1]{0:T(128)} %bitcast.place_ref, f32[8,32,256]{2,1,0:T(8,128)S(1)} %all-to-all-done.1.sums_ref, f32[256,256]{1,0:T(8,128)S(1)} %copy-done.1, s32[6,256]{1,0:T(8,128)S(1)} %get-tuple-element.30.rows_ref, ...), custom_call_target="tpu_custom_call" | custom-call | flops 6000000000 | bytes 1048576 | tf_op jit(solution)/shard_map/pallas_call | solution.py:380
  72.5 0.9 shard_map.34
  73.4 5.3 %all-to-all-start.3 = ((f32[8,64,256]{2,1,0:T(8,128)}), f32[8,64,256]{2,1,0:T(8,128)S(1)}, u32[]{:S(2)}, u32[]{:S(2)}) async-start(f32[8,64,256]{2,1,0:T(8,128)} %shard_map.34), calls=%async_computation.3 | async-start | bytes 1048576 | tf_op jit(solution)/shard_map/all_to_all | solution.py:109
  78.7 7.5 %collective-permute-start.2 = (f32[648,128]{1,0:T(8,128)S(1)}, f32[648,128]{1,0:T(8,128)S(1)}, u32[]{:S(2)}, u32[]{:S(2)}) collective-permute-start(f32[648,128]{1,0:T(8,128)S(1)} %get-tuple-element.17), channel_id=1, source_target_pairs={{0,0},{16,32},{32,16},{48,64},{64,48},{80,96},{96,80},{112,128},{1... | collective-permute-start | bytes 995336 | tf_op jit(solution)/shard_map/ppermute | solution.py:120
  86.2 2.1 %collective-permute-start.1 = (f32[648,128]{1,0:T(8,128)S(1)}, f32[648,128]{1,0:T(8,128)S(1)}, u32[]{:S(2)}, u32[]{:S(2)}) collective-permute-start(f32[648,128]{1,0:T(8,128)S(1)} %get-tuple-element.16.refs_0_), channel_id=1, source_target_pairs={{0,16},{16,0},{32,48},{48,32},{64,80},{80,64},{96,112},{112,96},{1... | collective-permute-start | bytes 995336 | tf_op jit(solution)/shard_map/ppermute | solution.py:114
  88.4 2.8 %collective-permute-done.2.outer_ref = f32[648,128]{1,0:T(8,128)S(1)} collective-permute-done((f32[648,128]{1,0:T(8,128)S(1)}, f32[648,128]{1,0:T(8,128)S(1)}, u32[]{:S(2)}, u32[]{:S(2)}) %collective-permute-start.2) | collective-permute-done | bytes 331808 | tf_op jit(solution)/shard_map/ppermute | solution.py:120
  91.3 7.4 %shard_map.35 = (f32[648,128]{1,0:T(8,128)S(1)}, f32[648,128]{1,0:T(8,128)S(1)}) custom-call(s32[1]{0:T(128)} %bitcast.place_ref, f32[648,128]{1,0:T(8,128)S(1)} %collective-permute-done.1.inner_ref, f32[648,128]{1,0:T(8,128)S(1)} %collective-permute-done.2.outer_ref, f32[8,64,256]{2,1,0:T(8,128)S(1)} %all-to-all-done.3.sums_ref, ...), custom_call_target="tpu_custom_call" | custom-call | flops 8000000000 | bytes 1048576 | tf_op jit(solution)/shard_map/pallas_call | solution.py:380
  98.7 11.2 %collective-permute-start.8 = (f32[648,128]{1,0:T(8,128)S(1)}, f32[648,128]{1,0:T(8,128)S(1)}, u32[]{:S(2)}, u32[]{:S(2)}) collective-permute-start(f32[648,128]{1,0:T(8,128)S(1)} %get-tuple-element.19), channel_id=1, source_target_pairs={{0,0},{16,32},{32,16},{48,64},{64,48},{80,96},{96,80},{112,128},{1... | collective-permute-start | bytes 995336 | tf_op jit(solution)/shard_map/ppermute | solution.py:120
  109.9 1.9 %collective-permute-start.9 = (f32[648,128]{1,0:T(8,128)S(1)}, f32[648,128]{1,0:T(8,128)S(1)}, u32[]{:S(2)}, u32[]{:S(2)}) collective-permute-start(f32[648,128]{1,0:T(8,128)S(1)} %get-tuple-element.20), channel_id=1, source_target_pairs={{0,16},{16,0},{32,48},{48,32},{64,80},{80,64},{96,112},{112,96},{1... | collective-permute-start | bytes 995336 | tf_op jit(solution)/shard_map/ppermute | solution.py:114
  112.0 2.7 %collective-permute-done.8.outer_ref = f32[648,128]{1,0:T(8,128)S(1)} collective-permute-done((f32[648,128]{1,0:T(8,128)S(1)}, f32[648,128]{1,0:T(8,128)S(1)}, u32[]{:S(2)}, u32[]{:S(2)}) %collective-permute-start.8) | collective-permute-done | bytes 331808 | tf_op jit(solution)/shard_map/ppermute | solution.py:120
  114.7 0.9 copy-done.3
  115.6 6.7 %shard_map.36 = (f32[256,128]{1,0:T(8,128)S(1)}, f32[256,128]{1,0:T(8,128)S(1)}) custom-call(s32[1]{0:T(128)} %bitcast.place_ref, f32[648,128]{1,0:T(8,128)S(1)} %collective-permute-done.8.outer_ref, f32[648,128]{1,0:T(8,128)S(1)} %collective-permute-done.9.inner_ref, f32[8,64,256]{2,1,0:T(8,128)S(1)} %all-to-all-done.3.sums_ref, f32[256,256]{1,0:T(8,128)S(1)} %copy-done.3, ...), custom_call_target="tpu_custom_call" | custom-call | flops 8000000000 | bytes 1048576 | tf_op jit(solution)/shard_map/pallas_call | solution.py:380
  122.3 5.8 %collective-permute-start.10 = (f32[256,128]{1,0:T(8,128)S(1)}, f32[256,128]{1,0:T(8,128)S(1)}, u32[]{:S(2)}, u32[]{:S(2)}) collective-permute-start(f32[256,128]{1,0:T(8,128)S(1)} %get-tuple-element.25), channel_id=1, source_target_pairs={{0,0},{16,32},{32,16},{48,64},{64,48},{80,96},{96,80},{112,128},{1... | collective-permute-start | bytes 393224 | tf_op jit(solution)/shard_map/ppermute | solution.py:120
  128.1 1.9 %collective-permute-start.11 = (f32[256,128]{1,0:T(8,128)S(1)}, f32[256,128]{1,0:T(8,128)S(1)}, u32[]{:S(2)}, u32[]{:S(2)}) collective-permute-start(f32[256,128]{1,0:T(8,128)S(1)} %get-tuple-element.26), channel_id=1, source_target_pairs={{0,16},{16,0},{32,48},{48,32},{64,80},{80,64},{96,112},{112,96},{1... | collective-permute-start | bytes 393224 | tf_op jit(solution)/shard_map/ppermute | solution.py:114
  (25 shorter events, 3.9 us)
Async XLA Ops:
  0.0 0.9 copy-start
  2.1 7.0 %copy-start.1 = (f32[256,256]{1,0:T(8,128)S(1)}, f32[256,256]{1,0:T(8,128)}, u32[]{:S(2)}) copy-start(f32[256,256]{1,0:T(8,128)} %block_ref.3) | copy-start | bytes 786436
  2.1 29.0 %all-to-all-start = ((f32[8,32,256]{2,1,0:T(8,128)}), f32[8,32,256]{2,1,0:T(8,128)S(1)}, u32[]{:S(2)}, u32[]{:S(2)}) async-start(f32[8,32,256]{2,1,0:T(8,128)} %shard_map.28), calls=%async_computation | async-start | bytes 524288 | tf_op jit(solution)/shard_map/all_to_all | solution.py:109
  9.0 12.0 %collective-permute-start.4 = (f32[256,256]{1,0:T(8,128)S(1)}, f32[256,256]{1,0:T(8,128)S(1)}, u32[]{:S(2)}, u32[]{:S(2)}) collective-permute-start(f32[256,256]{1,0:T(8,128)S(1)} %copy-done.1), channel_id=1, source_target_pairs={{0,16},{16,0},{32,48},{48,32},{64,80},{80,64},{96,112},{112,96},{1... | collective-permute-start | bytes 786440 | tf_op jit(solution)/shard_map/ppermute | solution.py:114
  11.9 9.8 %collective-permute-start.3 = (f32[256,256]{1,0:T(8,128)S(1)}, f32[256,256]{1,0:T(8,128)S(1)}, u32[]{:S(2)}, u32[]{:S(2)}) collective-permute-start(f32[256,256]{1,0:T(8,128)S(1)} %copy-done.1), channel_id=1, source_target_pairs={{0,0},{16,32},{32,16},{48,64},{64,48},{80,96},{96,80},{112,128},{1... | collective-permute-start | bytes 786440 | tf_op jit(solution)/shard_map/ppermute | solution.py:120
  15.7 9.4 %collective-permute-start.6 = (f32[256,256]{1,0:T(8,128)S(1)}, f32[256,256]{1,0:T(8,128)S(1)}, u32[]{:S(2)}, u32[]{:S(2)}) collective-permute-start(f32[256,256]{1,0:T(8,128)S(1)} %copy-done.1), channel_id=1, source_target_pairs={{0,32},{16,48},{32,64},{48,80},{64,96},{80,112},{96,128},{112,144}... | collective-permute-start | bytes 786440 | tf_op jit(solution)/shard_map/ppermute | solution.py:18
  18.9 10.7 %collective-permute-start.5 = (f32[256,256]{1,0:T(8,128)S(1)}, f32[256,256]{1,0:T(8,128)S(1)}, u32[]{:S(2)}, u32[]{:S(2)}) collective-permute-start(f32[256,256]{1,0:T(8,128)S(1)} %copy-done.1), channel_id=1, source_target_pairs={{32,0},{48,16},{64,32},{80,48},{96,64},{112,80},{128,96},{144,112}... | collective-permute-start | bytes 786440 | tf_op jit(solution)/shard_map/ppermute | solution.py:18
  31.1 22.1 %all-to-all-start.2 = ((f32[8,64,256]{2,1,0:T(8,128)}), f32[8,64,256]{2,1,0:T(8,128)S(1)}, u32[]{:S(2)}, u32[]{:S(2)}) async-start(f32[8,64,256]{2,1,0:T(8,128)} %get-tuple-element.18), calls=%async_computation.2 | async-start | bytes 1048576 | tf_op jit(solution)/shard_map/all_to_all | solution.py:109
  38.0 10.1 %collective-permute-start = (f32[32,256]{1,0:T(8,128)S(1)}, f32[32,256]{1,0:T(8,128)S(1)}, u32[]{:S(2)}, u32[]{:S(2)}) collective-permute-start(f32[32,256]{1,0:T(8,128)S(1)} %shard_map.29.one_ref), channel_id=1, source_target_pairs={{0,1},{1,0},{2,3},{3,2},{4,5},{5,4},{6,7},{7,6},{8,9},{9,8},{10,11... | collective-permute-start | bytes 98312 | tf_op jit(solution)/shard_map/ppermute | solution.py:395
  48.9 7.7 %copy-start.4 = (s32[3,6,256]{2,1,0:T(8,128)S(1)}, s32[3,6,256]{2,1,0:T(8,128)}, u32[]{:S(2)}) copy-start(s32[3,6,256]{2,1,0:T(8,128)} %param.3) | copy-start | bytes 55300
  53.2 12.8 %all-to-all-start.1 = ((f32[8,32,256]{2,1,0:T(8,128)}), f32[8,32,256]{2,1,0:T(8,128)S(1)}, u32[]{:S(2)}, u32[]{:S(2)}) async-start(f32[8,32,256]{2,1,0:T(8,128)} %shard_map.30), calls=%async_computation.1 | async-start | bytes 524288 | tf_op jit(solution)/shard_map/all_to_all | solution.py:109
  56.8 15.7 %collective-permute-start.7 = (f32[64,256]{1,0:T(8,128)S(1)}, f32[64,256]{1,0:T(8,128)S(1)}, u32[]{:S(2)}, u32[]{:S(2)}) collective-permute-start(f32[64,256]{1,0:T(8,128)S(1)} %shard_map.33.one_ref), channel_id=1, source_target_pairs={{0,1},{1,0},{2,3},{3,2},{4,5},{5,4},{6,7},{7,6},{8,9},{9,8},{10,11... | collective-permute-start | bytes 196616 | tf_op jit(solution)/shard_map/ppermute | solution.py:395
  71.8 0.7 copy-start.2
  73.4 17.9 %all-to-all-start.3 = ((f32[8,64,256]{2,1,0:T(8,128)}), f32[8,64,256]{2,1,0:T(8,128)S(1)}, u32[]{:S(2)}, u32[]{:S(2)}) async-start(f32[8,64,256]{2,1,0:T(8,128)} %shard_map.34), calls=%async_computation.3 | async-start | bytes 1048576 | tf_op jit(solution)/shard_map/all_to_all | solution.py:109
  78.7 12.6 %collective-permute-start.2 = (f32[648,128]{1,0:T(8,128)S(1)}, f32[648,128]{1,0:T(8,128)S(1)}, u32[]{:S(2)}, u32[]{:S(2)}) collective-permute-start(f32[648,128]{1,0:T(8,128)S(1)} %get-tuple-element.17), channel_id=1, source_target_pairs={{0,0},{16,32},{32,16},{48,64},{64,48},{80,96},{96,80},{112,128},{1... | collective-permute-start | bytes 995336 | tf_op jit(solution)/shard_map/ppermute | solution.py:120
  86.2 5.1 %collective-permute-start.1 = (f32[648,128]{1,0:T(8,128)S(1)}, f32[648,128]{1,0:T(8,128)S(1)}, u32[]{:S(2)}, u32[]{:S(2)}) collective-permute-start(f32[648,128]{1,0:T(8,128)S(1)} %get-tuple-element.16.refs_0_), channel_id=1, source_target_pairs={{0,16},{16,0},{32,48},{48,32},{64,80},{80,64},{96,112},{112,96},{1... | collective-permute-start | bytes 995336 | tf_op jit(solution)/shard_map/ppermute | solution.py:114
  98.7 16.0 %collective-permute-start.8 = (f32[648,128]{1,0:T(8,128)S(1)}, f32[648,128]{1,0:T(8,128)S(1)}, u32[]{:S(2)}, u32[]{:S(2)}) collective-permute-start(f32[648,128]{1,0:T(8,128)S(1)} %get-tuple-element.19), channel_id=1, source_target_pairs={{0,0},{16,32},{32,16},{48,64},{64,48},{80,96},{96,80},{112,128},{1... | collective-permute-start | bytes 995336 | tf_op jit(solution)/shard_map/ppermute | solution.py:120
  109.9 4.8 %collective-permute-start.9 = (f32[648,128]{1,0:T(8,128)S(1)}, f32[648,128]{1,0:T(8,128)S(1)}, u32[]{:S(2)}, u32[]{:S(2)}) collective-permute-start(f32[648,128]{1,0:T(8,128)S(1)} %get-tuple-element.20), channel_id=1, source_target_pairs={{0,16},{16,0},{32,48},{48,32},{64,80},{80,64},{96,112},{112,96},{1... | collective-permute-start | bytes 995336 | tf_op jit(solution)/shard_map/ppermute | solution.py:114
  114.7 1.0 copy-start.3
  122.3 8.4 %collective-permute-start.10 = (f32[256,128]{1,0:T(8,128)S(1)}, f32[256,128]{1,0:T(8,128)S(1)}, u32[]{:S(2)}, u32[]{:S(2)}) collective-permute-start(f32[256,128]{1,0:T(8,128)S(1)} %get-tuple-element.25), channel_id=1, source_target_pairs={{0,0},{16,32},{32,16},{48,64},{64,48},{80,96},{96,80},{112,128},{1... | collective-permute-start | bytes 393224 | tf_op jit(solution)/shard_map/ppermute | solution.py:120
  128.1 3.2 %collective-permute-start.11 = (f32[256,128]{1,0:T(8,128)S(1)}, f32[256,128]{1,0:T(8,128)S(1)}, u32[]{:S(2)}, u32[]{:S(2)}) collective-permute-start(f32[256,128]{1,0:T(8,128)S(1)} %get-tuple-element.26), channel_id=1, source_target_pairs={{0,16},{16,0},{32,48},{48,32},{64,80},{80,64},{96,112},{112,96},{1... | collective-permute-start | bytes 393224 | tf_op jit(solution)/shard_map/ppermute | solution.py:114

commit v5 on v4

--- a/solution.py
+++ b/solution.py
@@ -34,12 +34,25 @@
     return high + (middle + low)
 
 
+def two_parts(x):
+    return three_parts(x)[:2]
+
+
+def off_diagonal_by(x, diagonal, pick):
+    rows, few = x.shape[0], diagonal.shape[0]
+    dims = (((1,), (0,)), ((), ()))
+    stacked = jnp.concatenate(two_parts(x) + three_parts(diagonal), axis=0)
+    moved = lax.dot_general(stacked, pick, dims, preferred_element_type=F32)
+    high, middle, low = [moved[2 * rows + i * few : 2 * rows + (i + 1) * few] for i in range(3)]
+    return moved[:rows] + moved[rows : 2 * rows], high + (middle + low)
+
+
 def flipped_by(x, pick_t):
     dims = (((1,), (1,)), ((), ()))
-    high, middle, low = [
-        lax.dot_general(pick_t, part, dims, preferred_element_type=F32) for part in three_parts(x)
+    high, middle = [
+        lax.dot_general(pick_t, part, dims, preferred_element_type=F32) for part in two_parts(x)
     ]
-    return high + (middle + low)
+    return high + middle
 
 
 def rotation_of(a, b, g):
@@ -78,29 +91,34 @@
     rounds = len(rows)
     plain_row = lax.broadcasted_iota(jnp.int32, (1, width), 1)
     plain_column = lax.broadcasted_iota(jnp.int32, (width, 1), 0)
-    eye = lax.broadcasted_iota(jnp.int32, (half, half), 0) == lax.broadcasted_iota(
-        jnp.int32, (half, half), 1
-    )
+    on_diagonal = plain_row == plain_column
+    eye = on_diagonal[:half, :half]
     rows = [plain_row] + rows + [plain_row]
     columns = [plain_column] + columns + [plain_column]
 
-    def diagonal(block):
-        return jnp.sum(jnp.where(eye, block, 0.0), axis=0, keepdims=True)
-
-    gram = columns_by(
-        flipped_by(gram, one_hot(columns[1], rows[0])), one_hot(columns[0], rows[1])
+    diagonal = jnp.sum(jnp.where(on_diagonal, gram, 0.0), axis=0, keepdims=True)
+    gram = flipped_by(jnp.where(on_diagonal, 0.0, gram), one_hot(columns[1], rows[0]))
+    gram, diagonal = off_diagonal_by(
+        gram, jnp.broadcast_to(diagonal, (16, width)), one_hot(columns[0], rows[1])
     )
     rotation = jnp.where(plain_column == rows[1], 1.0, 0.0).astype(F32)
     for r in range(1, rounds + 1):
-        c, t = rotation_of(
-            diagonal(gram[:half, :half]), diagonal(gram[half:, half:]), diagonal(gram[:half, half:])
-        )
+        a, b = diagonal[:1, :half], diagonal[:1, half:]
+        g = jnp.sum(jnp.where(eye, gram[:half, half:], 0.0), axis=0, keepdims=True)
+        c, t = rotation_of(a, b, g)
         pick = one_hot(columns[r], rows[r + 1])
         if r < rounds or want_gram:
             pick_t = one_hot(columns[r + 1], rows[r])
-            gram = columns_by(turned(flipped_by(turned(gram, c, t), pick_t), c, t), pick)
+            partners = jnp.concatenate([rows[r][:, half:], rows[r][:, :half]], axis=1)
+            settled = (columns[r + 1] == rows[r]) | (columns[r + 1] == partners)
+            gram = turned(flipped_by(turned(gram, c, t), pick_t), c, t)
+            moved = t * (t * (b - a) - 2.0 * (c * g))
+            diagonal = jnp.broadcast_to(
+                jnp.concatenate([a + moved, b - moved], axis=1), (16, width)
+            )
+            gram, diagonal = off_diagonal_by(jnp.where(settled, 0.0, gram), diagonal, pick)
         rotation = columns_by(turned(rotation, c, t), pick)
-    return gram, rotation
+    return jnp.where(on_diagonal, diagonal[:1], gram), rotation
 
 
 def along_ring(parts):

time: 134 us -> 132 us (0.985)
  Pallas kernels: 24.2 us -> 22.1 us
    pallas_call x9, Pallas kernels: 24.2 us -> 22.1 us  [call(): pl.pallas_call(kernel, out_shape=shapes, in_specs=[spec for _, spec in op...]
where the time goes in v5:
time: 132 us; the launch traced here: 130 us
  starting transfers between devices  81.7 us (62%)
  waiting for transfers between devices  22.2 us (17%)
  Pallas kernels  22.1 us (17%)
  local copies, waits for them, and re-layouts  3.01 us (2%)
    ppermute x4, starting transfers between devices, outer_swap(): return lax.ppermute(array, 'col', pairs)  28.3 us
    all_to_all x4, starting transfers between devices, along_ring(): return lax.all_to_all(parts, 'row', 0, 0, axis_index_groups=rings)  22.6 us
    pallas_call x9, Pallas kernels, call(): pl.pallas_call(kernel, out_shape=shapes, in_specs=[spec for _, spec in op...  22.1 us
    ppermute x2, starting transfers between devices, reduced(): other = lax.ppermute(total, 'row', across)  16.7 us
    ppermute x4, starting transfers between devices, chip_swap(): return lax.ppermute(array, 'col', [(m, m ^ 1) for m in range(slots)])  8.81 us
    ppermute x2, waiting for transfers between devices, shifted(): return lax.ppermute(array, axis, pairs)  7.81 us
    ppermute x4, waiting for transfers between devices, outer_swap(): return lax.ppermute(array, 'col', pairs)  6.92 us
    all_to_all x4, waiting for transfers between devices, along_ring(): return lax.all_to_all(parts, 'row', 0, 0, axis_index_groups=rings)  5.54 us
  transfers between devices with their start and end apart: 16, of which 10 were waited for; matrix products, arithmetic and copies ran while one was open for 0% of the time, Pallas kernels for 6%

profile of v5, /device:TPU:7, one launch (start us, length us, event | category | flops | bytes accessed | tf_op | source)
XLA Modules:
  0.0 130.0 jit_solution(11374150175846954868)
XLA Ops:
  0.0 0.9 copy-done
  1.0 1.1 shard_map.28
  2.1 7.0 %all-to-all-start = ((f32[8,32,256]{2,1,0:T(8,128)}), f32[8,32,256]{2,1,0:T(8,128)S(1)}, u32[]{:S(2)}, u32[]{:S(2)}) async-start(f32[8,32,256]{2,1,0:T(8,128)} %shard_map.28), calls=%async_computation | async-start | bytes 524288 | tf_op jit(solution)/shard_map/all_to_all | solution.py:127
  9.0 2.9 %collective-permute-start.4 = (f32[256,256]{1,0:T(8,128)S(1)}, f32[256,256]{1,0:T(8,128)S(1)}, u32[]{:S(2)}, u32[]{:S(2)}) collective-permute-start(f32[256,256]{1,0:T(8,128)S(1)} %copy-done.1), channel_id=1, source_target_pairs={{0,16},{16,0},{32,48},{48,32},{64,80},{80,64},{96,112},{112,96},{1... | collective-permute-start | bytes 786440 | tf_op jit(solution)/shard_map/ppermute | solution.py:132
  11.9 3.8 %collective-permute-start.3 = (f32[256,256]{1,0:T(8,128)S(1)}, f32[256,256]{1,0:T(8,128)S(1)}, u32[]{:S(2)}, u32[]{:S(2)}) collective-permute-start(f32[256,256]{1,0:T(8,128)S(1)} %copy-done.1), channel_id=1, source_target_pairs={{0,0},{16,32},{32,16},{48,64},{64,48},{80,96},{96,80},{112,128},{1... | collective-permute-start | bytes 786440 | tf_op jit(solution)/shard_map/ppermute | solution.py:138
  15.7 3.1 %collective-permute-start.6 = (f32[256,256]{1,0:T(8,128)S(1)}, f32[256,256]{1,0:T(8,128)S(1)}, u32[]{:S(2)}, u32[]{:S(2)}) collective-permute-start(f32[256,256]{1,0:T(8,128)S(1)} %copy-done.1), channel_id=1, source_target_pairs={{0,32},{16,48},{32,64},{48,80},{64,96},{80,112},{96,128},{112,144}... | collective-permute-start | bytes 786440 | tf_op jit(solution)/shard_map/ppermute | solution.py:18
  18.9 2.2 %collective-permute-start.5 = (f32[256,256]{1,0:T(8,128)S(1)}, f32[256,256]{1,0:T(8,128)S(1)}, u32[]{:S(2)}, u32[]{:S(2)}) collective-permute-start(f32[256,256]{1,0:T(8,128)S(1)} %copy-done.1), channel_id=1, source_target_pairs={{32,0},{48,16},{64,32},{80,48},{96,64},{112,80},{128,96},{144,112}... | collective-permute-start | bytes 786440 | tf_op jit(solution)/shard_map/ppermute | solution.py:18
  21.7 3.4 %collective-permute-done.6.far_before_ref = f32[256,256]{1,0:T(8,128)S(1)} collective-permute-done((f32[256,256]{1,0:T(8,128)S(1)}, f32[256,256]{1,0:T(8,128)S(1)}, u32[]{:S(2)}, u32[]{:S(2)}) %collective-permute-start.6) | collective-permute-done | bytes 262176 | tf_op jit(solution)/shard_map/ppermute | solution.py:18
  25.2 4.4 %collective-permute-done.5.far_after_ref = f32[256,256]{1,0:T(8,128)S(1)} collective-permute-done((f32[256,256]{1,0:T(8,128)S(1)}, f32[256,256]{1,0:T(8,128)S(1)}, u32[]{:S(2)}, u32[]{:S(2)}) %collective-permute-start.5) | collective-permute-done | bytes 262176 | tf_op jit(solution)/shard_map/ppermute | solution.py:18
  29.5 1.6 %shard_map.32 = (f32[8,64,256]{2,1,0:T(8,128)}, f32[256,256]{1,0:T(8,128)S(1)}, f32[256,256]{1,0:T(8,128)S(1)}) custom-call(s32[1]{0:T(128)} %bitcast.place_ref, f32[256,256]{1,0:T(8,128)S(1)} %collective-permute-done.3.outer_ref, f32[256,256]{1,0:T(8,128)S(1)} %collective-permute-done.4.inner_ref, f32[256,256]{1,0:T(8,128)S(1)} %collective-permute-done.5.far_after_ref, ...), custom_call_target="tpu_custom_call" | custom-call | flops 2000000000 | bytes 1048576 | tf_op jit(solution)/shard_map/pallas_call | solution.py:398
  31.1 6.9 %all-to-all-start.2 = ((f32[8,64,256]{2,1,0:T(8,128)}), f32[8,64,256]{2,1,0:T(8,128)S(1)}, u32[]{:S(2)}, u32[]{:S(2)}) async-start(f32[8,64,256]{2,1,0:T(8,128)} %get-tuple-element.18), calls=%async_computation.2 | async-start | bytes 1048576 | tf_op jit(solution)/shard_map/all_to_all | solution.py:127
  38.0 8.8 %collective-permute-start = (f32[32,256]{1,0:T(8,128)S(1)}, f32[32,256]{1,0:T(8,128)S(1)}, u32[]{:S(2)}, u32[]{:S(2)}) collective-permute-start(f32[32,256]{1,0:T(8,128)S(1)} %shard_map.29.one_ref), channel_id=1, source_target_pairs={{0,1},{1,0},{2,3},{3,2},{4,5},{5,4},{6,7},{7,6},{8,9},{9,8},{10,11... | collective-permute-start | bytes 98312 | tf_op jit(solution)/shard_map/ppermute | solution.py:413
  46.9 1.3 collective-permute-done.other_ref
  48.2 0.7 shard_map.30
  48.9 4.3 %all-to-all-done.2.in_ref = f32[8,64,256]{2,1,0:T(8,128)S(1)} async-done(((f32[8,64,256]{2,1,0:T(8,128)}), f32[8,64,256]{2,1,0:T(8,128)S(1)}, u32[]{:S(2)}, u32[]{:S(2)}) %all-to-all-start.2) | async-done | bytes 524320 | tf_op jit(solution)/shard_map/all_to_all | solution.py:127
  53.2 3.4 %all-to-all-start.1 = ((f32[8,32,256]{2,1,0:T(8,128)}), f32[8,32,256]{2,1,0:T(8,128)S(1)}, u32[]{:S(2)}, u32[]{:S(2)}) async-start(f32[8,32,256]{2,1,0:T(8,128)} %shard_map.30), calls=%async_computation.1 | async-start | bytes 524288 | tf_op jit(solution)/shard_map/all_to_all | solution.py:127
  56.8 7.9 %collective-permute-start.7 = (f32[64,256]{1,0:T(8,128)S(1)}, f32[64,256]{1,0:T(8,128)S(1)}, u32[]{:S(2)}, u32[]{:S(2)}) collective-permute-start(f32[64,256]{1,0:T(8,128)S(1)} %shard_map.33.one_ref), channel_id=1, source_target_pairs={{0,1},{1,0},{2,3},{3,2},{4,5},{5,4},{6,7},{7,6},{8,9},{9,8},{10,11... | collective-permute-start | bytes 196616 | tf_op jit(solution)/shard_map/ppermute | solution.py:413
  64.7 1.3 all-to-all-done.1.sums_ref
  66.0 5.1 %shard_map.31 = (f32[648,128]{1,0:T(8,128)S(1)}, f32[648,128]{1,0:T(8,128)S(1)}, f32[256,256]{1,0:T(8,128)S(1)}, f32[128,128]{1,0:T(8,128)S(1)}) custom-call(s32[1]{0:T(128)} %bitcast.place_ref, f32[8,32,256]{2,1,0:T(8,128)S(1)} %all-to-all-done.1.sums_ref, f32[256,256]{1,0:T(8,128)S(1)} %copy-done.1, s32[6,256]{1,0:T(8,128)S(1)} %get-tuple-element.30.rows_ref, ...), custom_call_target="tpu_custom_call" | custom-call | flops 6000000000 | bytes 1048576 | tf_op jit(solution)/shard_map/pallas_call | solution.py:398
  71.8 0.9 shard_map.34
  72.7 5.3 %all-to-all-start.3 = ((f32[8,64,256]{2,1,0:T(8,128)}), f32[8,64,256]{2,1,0:T(8,128)S(1)}, u32[]{:S(2)}, u32[]{:S(2)}) async-start(f32[8,64,256]{2,1,0:T(8,128)} %shard_map.34), calls=%async_computation.3 | async-start | bytes 1048576 | tf_op jit(solution)/shard_map/all_to_all | solution.py:127
  77.9 7.5 %collective-permute-start.2 = (f32[648,128]{1,0:T(8,128)S(1)}, f32[648,128]{1,0:T(8,128)S(1)}, u32[]{:S(2)}, u32[]{:S(2)}) collective-permute-start(f32[648,128]{1,0:T(8,128)S(1)} %get-tuple-element.17), channel_id=1, source_target_pairs={{0,0},{16,32},{32,16},{48,64},{64,48},{80,96},{96,80},{112,128},{1... | collective-permute-start | bytes 995336 | tf_op jit(solution)/shard_map/ppermute | solution.py:138
  85.5 2.1 %collective-permute-start.1 = (f32[648,128]{1,0:T(8,128)S(1)}, f32[648,128]{1,0:T(8,128)S(1)}, u32[]{:S(2)}, u32[]{:S(2)}) collective-permute-start(f32[648,128]{1,0:T(8,128)S(1)} %get-tuple-element.16.refs_0_), channel_id=1, source_target_pairs={{0,16},{16,0},{32,48},{48,32},{64,80},{80,64},{96,112},{112,96},{1... | collective-permute-start | bytes 995336 | tf_op jit(solution)/shard_map/ppermute | solution.py:132
  87.7 2.8 %collective-permute-done.2.outer_ref = f32[648,128]{1,0:T(8,128)S(1)} collective-permute-done((f32[648,128]{1,0:T(8,128)S(1)}, f32[648,128]{1,0:T(8,128)S(1)}, u32[]{:S(2)}, u32[]{:S(2)}) %collective-permute-start.2) | collective-permute-done | bytes 331808 | tf_op jit(solution)/shard_map/ppermute | solution.py:138
  90.5 6.7 %shard_map.35 = (f32[648,128]{1,0:T(8,128)S(1)}, f32[648,128]{1,0:T(8,128)S(1)}) custom-call(s32[1]{0:T(128)} %bitcast.place_ref, f32[648,128]{1,0:T(8,128)S(1)} %collective-permute-done.1.inner_ref, f32[648,128]{1,0:T(8,128)S(1)} %collective-permute-done.2.outer_ref, f32[8,64,256]{2,1,0:T(8,128)S(1)} %all-to-all-done.3.sums_ref, ...), custom_call_target="tpu_custom_call" | custom-call | flops 8000000000 | bytes 1048576 | tf_op jit(solution)/shard_map/pallas_call | solution.py:398
  97.2 11.2 %collective-permute-start.8 = (f32[648,128]{1,0:T(8,128)S(1)}, f32[648,128]{1,0:T(8,128)S(1)}, u32[]{:S(2)}, u32[]{:S(2)}) collective-permute-start(f32[648,128]{1,0:T(8,128)S(1)} %get-tuple-element.19), channel_id=1, source_target_pairs={{0,0},{16,32},{32,16},{48,64},{64,48},{80,96},{96,80},{112,128},{1... | collective-permute-start | bytes 995336 | tf_op jit(solution)/shard_map/ppermute | solution.py:138
  108.4 1.9 %collective-permute-start.9 = (f32[648,128]{1,0:T(8,128)S(1)}, f32[648,128]{1,0:T(8,128)S(1)}, u32[]{:S(2)}, u32[]{:S(2)}) collective-permute-start(f32[648,128]{1,0:T(8,128)S(1)} %get-tuple-element.20), channel_id=1, source_target_pairs={{0,16},{16,0},{32,48},{48,32},{64,80},{80,64},{96,112},{112,96},{1... | collective-permute-start | bytes 995336 | tf_op jit(solution)/shard_map/ppermute | solution.py:132
  110.5 2.7 %collective-permute-done.8.outer_ref = f32[648,128]{1,0:T(8,128)S(1)} collective-permute-done((f32[648,128]{1,0:T(8,128)S(1)}, f32[648,128]{1,0:T(8,128)S(1)}, u32[]{:S(2)}, u32[]{:S(2)}) %collective-permute-start.8) | collective-permute-done | bytes 331808 | tf_op jit(solution)/shard_map/ppermute | solution.py:138
  113.2 0.9 copy-done.3
  114.2 6.1 %shard_map.36 = (f32[256,128]{1,0:T(8,128)S(1)}, f32[256,128]{1,0:T(8,128)S(1)}) custom-call(s32[1]{0:T(128)} %bitcast.place_ref, f32[648,128]{1,0:T(8,128)S(1)} %collective-permute-done.8.outer_ref, f32[648,128]{1,0:T(8,128)S(1)} %collective-permute-done.9.inner_ref, f32[8,64,256]{2,1,0:T(8,128)S(1)} %all-to-all-done.3.sums_ref, f32[256,256]{1,0:T(8,128)S(1)} %copy-done.3, ...), custom_call_target="tpu_custom_call" | custom-call | flops 8000000000 | bytes 1048576 | tf_op jit(solution)/shard_map/pallas_call | solution.py:398
  120.2 5.8 %collective-permute-start.10 = (f32[256,128]{1,0:T(8,128)S(1)}, f32[256,128]{1,0:T(8,128)S(1)}, u32[]{:S(2)}, u32[]{:S(2)}) collective-permute-start(f32[256,128]{1,0:T(8,128)S(1)} %get-tuple-element.25), channel_id=1, source_target_pairs={{0,0},{16,32},{32,16},{48,64},{64,48},{80,96},{96,80},{112,128},{1... | collective-permute-start | bytes 393224 | tf_op jit(solution)/shard_map/ppermute | solution.py:138
  126.0 1.9 %collective-permute-start.11 = (f32[256,128]{1,0:T(8,128)S(1)}, f32[256,128]{1,0:T(8,128)S(1)}, u32[]{:S(2)}, u32[]{:S(2)}) collective-permute-start(f32[256,128]{1,0:T(8,128)S(1)} %get-tuple-element.26), channel_id=1, source_target_pairs={{0,16},{16,0},{32,48},{48,32},{64,80},{80,64},{96,112},{112,96},{1... | collective-permute-start | bytes 393224 | tf_op jit(solution)/shard_map/ppermute | solution.py:132
  (25 shorter events, 3.9 us)
Async XLA Ops:
  0.0 0.9 copy-start
  2.1 7.0 %copy-start.1 = (f32[256,256]{1,0:T(8,128)S(1)}, f32[256,256]{1,0:T(8,128)}, u32[]{:S(2)}) copy-start(f32[256,256]{1,0:T(8,128)} %block_ref.3) | copy-start | bytes 786436
  2.1 29.0 %all-to-all-start = ((f32[8,32,256]{2,1,0:T(8,128)}), f32[8,32,256]{2,1,0:T(8,128)S(1)}, u32[]{:S(2)}, u32[]{:S(2)}) async-start(f32[8,32,256]{2,1,0:T(8,128)} %shard_map.28), calls=%async_computation | async-start | bytes 524288 | tf_op jit(solution)/shard_map/all_to_all | solution.py:127
  9.0 12.0 %collective-permute-start.4 = (f32[256,256]{1,0:T(8,128)S(1)}, f32[256,256]{1,0:T(8,128)S(1)}, u32[]{:S(2)}, u32[]{:S(2)}) collective-permute-start(f32[256,256]{1,0:T(8,128)S(1)} %copy-done.1), channel_id=1, source_target_pairs={{0,16},{16,0},{32,48},{48,32},{64,80},{80,64},{96,112},{112,96},{1... | collective-permute-start | bytes 786440 | tf_op jit(solution)/shard_map/ppermute | solution.py:132
  11.9 9.8 %collective-permute-start.3 = (f32[256,256]{1,0:T(8,128)S(1)}, f32[256,256]{1,0:T(8,128)S(1)}, u32[]{:S(2)}, u32[]{:S(2)}) collective-permute-start(f32[256,256]{1,0:T(8,128)S(1)} %copy-done.1), channel_id=1, source_target_pairs={{0,0},{16,32},{32,16},{48,64},{64,48},{80,96},{96,80},{112,128},{1... | collective-permute-start | bytes 786440 | tf_op jit(solution)/shard_map/ppermute | solution.py:138
  15.7 9.4 %collective-permute-start.6 = (f32[256,256]{1,0:T(8,128)S(1)}, f32[256,256]{1,0:T(8,128)S(1)}, u32[]{:S(2)}, u32[]{:S(2)}) collective-permute-start(f32[256,256]{1,0:T(8,128)S(1)} %copy-done.1), channel_id=1, source_target_pairs={{0,32},{16,48},{32,64},{48,80},{64,96},{80,112},{96,128},{112,144}... | collective-permute-start | bytes 786440 | tf_op jit(solution)/shard_map/ppermute | solution.py:18
  18.9 10.7 %collective-permute-start.5 = (f32[256,256]{1,0:T(8,128)S(1)}, f32[256,256]{1,0:T(8,128)S(1)}, u32[]{:S(2)}, u32[]{:S(2)}) collective-permute-start(f32[256,256]{1,0:T(8,128)S(1)} %copy-done.1), channel_id=1, source_target_pairs={{32,0},{48,16},{64,32},{80,48},{96,64},{112,80},{128,96},{144,112}... | collective-permute-start | bytes 786440 | tf_op jit(solution)/shard_map/ppermute | solution.py:18
  31.1 22.1 %all-to-all-start.2 = ((f32[8,64,256]{2,1,0:T(8,128)}), f32[8,64,256]{2,1,0:T(8,128)S(1)}, u32[]{:S(2)}, u32[]{:S(2)}) async-start(f32[8,64,256]{2,1,0:T(8,128)} %get-tuple-element.18), calls=%async_computation.2 | async-start | bytes 1048576 | tf_op jit(solution)/shard_map/all_to_all | solution.py:127
  38.0 10.1 %collective-permute-start = (f32[32,256]{1,0:T(8,128)S(1)}, f32[32,256]{1,0:T(8,128)S(1)}, u32[]{:S(2)}, u32[]{:S(2)}) collective-permute-start(f32[32,256]{1,0:T(8,128)S(1)} %shard_map.29.one_ref), channel_id=1, source_target_pairs={{0,1},{1,0},{2,3},{3,2},{4,5},{5,4},{6,7},{7,6},{8,9},{9,8},{10,11... | collective-permute-start | bytes 98312 | tf_op jit(solution)/shard_map/ppermute | solution.py:413
  48.9 7.7 %copy-start.4 = (s32[3,6,256]{2,1,0:T(8,128)S(1)}, s32[3,6,256]{2,1,0:T(8,128)}, u32[]{:S(2)}) copy-start(s32[3,6,256]{2,1,0:T(8,128)} %param.3) | copy-start | bytes 55300
  53.2 12.8 %all-to-all-start.1 = ((f32[8,32,256]{2,1,0:T(8,128)}), f32[8,32,256]{2,1,0:T(8,128)S(1)}, u32[]{:S(2)}, u32[]{:S(2)}) async-start(f32[8,32,256]{2,1,0:T(8,128)} %shard_map.30), calls=%async_computation.1 | async-start | bytes 524288 | tf_op jit(solution)/shard_map/all_to_all | solution.py:127
  56.8 15.0 %collective-permute-start.7 = (f32[64,256]{1,0:T(8,128)S(1)}, f32[64,256]{1,0:T(8,128)S(1)}, u32[]{:S(2)}, u32[]{:S(2)}) collective-permute-start(f32[64,256]{1,0:T(8,128)S(1)} %shard_map.33.one_ref), channel_id=1, source_target_pairs={{0,1},{1,0},{2,3},{3,2},{4,5},{5,4},{6,7},{7,6},{8,9},{9,8},{10,11... | collective-permute-start | bytes 196616 | tf_op jit(solution)/shard_map/ppermute | solution.py:413
  71.1 0.7 copy-start.2
  72.7 17.9 %all-to-all-start.3 = ((f32[8,64,256]{2,1,0:T(8,128)}), f32[8,64,256]{2,1,0:T(8,128)S(1)}, u32[]{:S(2)}, u32[]{:S(2)}) async-start(f32[8,64,256]{2,1,0:T(8,128)} %shard_map.34), calls=%async_computation.3 | async-start | bytes 1048576 | tf_op jit(solution)/shard_map/all_to_all | solution.py:127
  77.9 12.6 %collective-permute-start.2 = (f32[648,128]{1,0:T(8,128)S(1)}, f32[648,128]{1,0:T(8,128)S(1)}, u32[]{:S(2)}, u32[]{:S(2)}) collective-permute-start(f32[648,128]{1,0:T(8,128)S(1)} %get-tuple-element.17), channel_id=1, source_target_pairs={{0,0},{16,32},{32,16},{48,64},{64,48},{80,96},{96,80},{112,128},{1... | collective-permute-start | bytes 995336 | tf_op jit(solution)/shard_map/ppermute | solution.py:138
  85.5 5.1 %collective-permute-start.1 = (f32[648,128]{1,0:T(8,128)S(1)}, f32[648,128]{1,0:T(8,128)S(1)}, u32[]{:S(2)}, u32[]{:S(2)}) collective-permute-start(f32[648,128]{1,0:T(8,128)S(1)} %get-tuple-element.16.refs_0_), channel_id=1, source_target_pairs={{0,16},{16,0},{32,48},{48,32},{64,80},{80,64},{96,112},{112,96},{1... | collective-permute-start | bytes 995336 | tf_op jit(solution)/shard_map/ppermute | solution.py:132
  97.2 16.0 %collective-permute-start.8 = (f32[648,128]{1,0:T(8,128)S(1)}, f32[648,128]{1,0:T(8,128)S(1)}, u32[]{:S(2)}, u32[]{:S(2)}) collective-permute-start(f32[648,128]{1,0:T(8,128)S(1)} %get-tuple-element.19), channel_id=1, source_target_pairs={{0,0},{16,32},{32,16},{48,64},{64,48},{80,96},{96,80},{112,128},{1... | collective-permute-start | bytes 995336 | tf_op jit(solution)/shard_map/ppermute | solution.py:138
  108.4 4.8 %collective-permute-start.9 = (f32[648,128]{1,0:T(8,128)S(1)}, f32[648,128]{1,0:T(8,128)S(1)}, u32[]{:S(2)}, u32[]{:S(2)}) collective-permute-start(f32[648,128]{1,0:T(8,128)S(1)} %get-tuple-element.20), channel_id=1, source_target_pairs={{0,16},{16,0},{32,48},{48,32},{64,80},{80,64},{96,112},{112,96},{1... | collective-permute-start | bytes 995336 | tf_op jit(solution)/shard_map/ppermute | solution.py:132
  113.2 1.0 copy-start.3
  120.2 8.4 %collective-permute-start.10 = (f32[256,128]{1,0:T(8,128)S(1)}, f32[256,128]{1,0:T(8,128)S(1)}, u32[]{:S(2)}, u32[]{:S(2)}) collective-permute-start(f32[256,128]{1,0:T(8,128)S(1)} %get-tuple-element.25), channel_id=1, source_target_pairs={{0,0},{16,32},{32,16},{48,64},{64,48},{80,96},{96,80},{112,128},{1... | collective-permute-start | bytes 393224 | tf_op jit(solution)/shard_map/ppermute | solution.py:138
  126.0 3.2 %collective-permute-start.11 = (f32[256,128]{1,0:T(8,128)S(1)}, f32[256,128]{1,0:T(8,128)S(1)}, u32[]{:S(2)}, u32[]{:S(2)}) collective-permute-start(f32[256,128]{1,0:T(8,128)S(1)} %get-tuple-element.26), channel_id=1, source_target_pairs={{0,16},{16,0},{32,48},{48,32},{64,80},{80,64},{96,112},{112,96},{1... | collective-permute-start | bytes 393224 | tf_op jit(solution)/shard_map/ppermute | solution.py:132
